TPU v7x, 768 devices: a whole 4x8x12 slice. The times are simulated.
768 devices in a mesh: nodes: 96 (over x, z, core), cols: 8 (over y).
Axes of the slice: x: 4, y: 8, z: 12, core: 2. Of those that a mesh axis runs over, the one named last changes fastest.
Arguments:
- features: bfloat16 [98304, 1024], P('nodes'), may hold values from -6 to 6
- w_self: bfloat16 [1024, 1024], P(None, 'cols'), may hold values from -1 to 1
- w_neigh: bfloat16 [1024, 1024], P(None, 'cols'), may hold values from -1 to 1
- local_nbr: int32 [98304, 8], P('nodes'), may hold values from 0 to 1023
- hub_link: int32 [98304, 4], P('nodes'), may hold values from 0 to 767
- hub_used: int32 [98304, 4], P('nodes'), may hold values 0 or 1
- cotangent: bfloat16 [98304, 1024], P('nodes', 'cols'), may hold values from -0.046875 to 0.046875
Outputs:
- output: bfloat16 [98304, 1024], P('nodes', 'cols')
- grad_self: float32 [1024, 1024], P(None, 'cols')
- grad_neigh: float32 [1024, 1024], P(None, 'cols')
All inputs are finite; a program needn't handle non-finite values. No bound on the sum of `hub_used` on one device may be relied on, other than what follows from the above.
Results may differ from a plain program's by a relative error of at most 0.007.
Values may be sent and summed in bfloat16 or wider, within the bound.
A program may use at most 32 MiB of HBM per device.

v0:
```python
import jax
import jax.numpy as jnp
from jax import lax
from jax.sharding import PartitionSpec as P

D = 1024
HUB_DEV = 8
FAN = 8


epsilon = 1e-05


def column_total(values):
    return lax.psum(values, "cols")


def hub_parts(values, hub_link, used_mask, count_part):
    row_count, col_width = values.shape
    link_count = hub_link.shape[1]
    total_hubs = HUB_DEV * lax.axis_size("nodes")
    own_hubs = values[:HUB_DEV]
    piece = lax.all_gather(own_hubs, "nodes", axis=0, tiled=True)
    piece_rows = piece.shape[0]
    slots = jnp.arange(piece_rows, dtype=jnp.int32)
    linked = jnp.zeros((row_count, piece_rows), jnp.float32)
    for k in range(link_count):
        linked = linked + jnp.where(
            hub_link[:, k][:, None] == slots[None, :], used_mask[:, k][:, None], 0.0
        )
    pulled = jnp.dot(linked.astype(jnp.bfloat16), piece, preferred_element_type=jnp.float32)
    spread = (values.astype(jnp.float32)[:, None, :] * used_mask[:, :, None]).reshape(
        row_count * link_count, col_width
    )
    pushed = jax.ops.segment_sum(spread, hub_link.reshape(-1), num_segments=total_hubs)
    inflow, count_in = (
        lax.psum_scatter(pushed, "nodes", scatter_dimension=0, tiled=True),
        lax.psum_scatter(count_part, "nodes", scatter_dimension=0, tiled=True),
    )
    inflow = jnp.pad(inflow, ((0, row_count - HUB_DEV), (0, 0)))
    count_in = jnp.pad(count_in, (0, row_count - HUB_DEV))
    return (pulled + inflow, count_in)


def local(features, w_self, w_neigh, local_nbr, hub_link, hub_used, cotangent):
    row_count = features.shape[0]
    col_width = w_self.shape[1]
    fanout = local_nbr.shape[1]
    total_hubs = HUB_DEV * lax.axis_size("nodes")
    contract = (((0,), (0,)), ((), ()))
    used_mask = hub_used.astype(jnp.float32)
    count_part = jax.ops.segment_sum(
        used_mask.reshape(-1), hub_link.reshape(-1), num_segments=total_hubs
    )
    proj_self = jnp.dot(features, w_self, preferred_element_type=jnp.float32)
    proj_neigh = jnp.dot(features, w_neigh, preferred_element_type=jnp.float32).astype(jnp.bfloat16)
    hub_sum, count_in = hub_parts(proj_neigh, hub_link, used_mask, count_part)
    local_sum = jnp.zeros((row_count, col_width), jnp.float32)
    for k in range(fanout):
        local_sum = local_sum + jnp.take(proj_neigh, local_nbr[:, k], axis=0).astype(jnp.float32)
    degree = FAN + jnp.sum(used_mask, axis=1) + count_in
    pre_act = proj_self + (local_sum + hub_sum) / degree[:, None]
    sig_gate = jax.nn.sigmoid(pre_act)
    activated = pre_act * sig_gate
    cot_values = cotangent.astype(jnp.float32)
    row_scale = jnp.sqrt(column_total(jnp.sum(activated * activated, axis=1)) / D + epsilon)
    normed = activated / row_scale[:, None]
    inner_mean = column_total(jnp.sum(cot_values * normed, axis=1)) / D
    output = normed.astype(jnp.bfloat16)
    act_slope = sig_gate * (1.0 + pre_act * (1.0 - sig_gate))
    grad_pre = (cot_values - normed * inner_mean[:, None]) / row_scale[:, None] * act_slope
    grad_low = grad_pre.astype(jnp.bfloat16)
    scaled_grad = (grad_pre / degree[:, None]).astype(jnp.bfloat16)
    hub_back, spare_count = hub_parts(scaled_grad, hub_link, used_mask, count_part)
    scaled_f32 = scaled_grad.astype(jnp.float32)
    repeated = jnp.broadcast_to(scaled_f32[:, None, :], (row_count, fanout, col_width)).reshape(
        row_count * fanout, col_width
    )
    back_local = jax.ops.segment_sum(repeated, local_nbr.reshape(-1), num_segments=row_count)
    back_agg = (back_local + hub_back).astype(jnp.bfloat16)
    neigh_part = lax.dot_general(features, back_agg, contract, preferred_element_type=jnp.float32)
    self_part = lax.dot_general(features, grad_low, contract, preferred_element_type=jnp.float32)
    grad_self, grad_neigh = lax.psum((self_part, neigh_part), "nodes")
    return (output, grad_self, grad_neigh)


def solution(mesh):
    placed = (
        P("nodes", None),
        P(None, "cols"),
        P(None, "cols"),
        P("nodes", None),
        P("nodes", None),
        P("nodes", None),
        P("nodes", "cols"),
    )
    return jax.shard_map(
        local,
        mesh=mesh,
        in_specs=placed,
        out_specs=(P("nodes", "cols"), P(None, "cols"), P(None, "cols")),
        check_vma=False,
    )
```

profile of v0, /device:TPU:1, one launch (start us, length us, event | category | flops | bytes accessed | tf_op | source)
XLA Modules:
  0.0 1114.5 jit_solution(10795895139459330795)
XLA Ops:
  12.2 25.5 %scatter_custom_fusion = f32[768,128]{1,0:T(8,128)} fusion(s32[4096]{0:T(1024)S(1)} %reshape.95, f32[4096,128]{1,0:T(8,128)} %bitcast.36, f32[4096]{0:T(1024)S(1)} %reshape.105, f32[]{:T(128)} %constant.13.clone.1), kind=kCustom, calls=%fused_computation.22 | custom fusion | flops 1048576 | bytes 2506756 | tf_op jit(solution)/shard_map/scatter-add | solution.py:35
  37.7 28.8 %scatter_custom_fusion.1 = f32[768]{0:T(1024)S(1)} fusion(s32[4096]{0:T(1024)S(1)} %reshape.95, f32[4096]{0:T(1024)S(1)} %reshape.105, f32[]{:T(128)} %constant.13.clone.1), kind=kCustom, calls=%fused_computation.75 | custom fusion | flops 4096 | bytes 3076 | tf_op jit(solution)/shard_map/scatter-add | solution.py:52
  67.0 196.3 %all-reduce.4 = f32[768]{0:T(1024)S(1)} all-reduce(f32[768]{0:T(1024)S(1)} %scatter_custom_fusion.1), channel_id=3, replica_groups=mesh['nodes'=96,'cols'=8] {'nodes'}, use_global_device_ids=true, to_apply=%region_4.6.clone | all-reduce | flops 768 | bytes 6144
  263.3 82.9 %all_gather.6 = bf16[768,128]{1,0:T(8,128)(2,1)} all-gather(bf16[8,128]{1,0:T(8,128)(2,1)S(1)} %slice.100), channel_id=1, replica_groups=mesh['nodes'=96,'cols'=8] {'nodes'}, dimensions={0}, use_global_device_ids=true | all-gather | bytes 198656 | tf_op jit(solution)/shard_map/all_gather | solution.py:23
  346.1 3.2 gather_fusion.7
  349.3 3.2 gather_fusion.6
  352.6 4.3 gather_fusion.5
  356.9 4.3 gather_fusion.4
  361.2 4.3 gather_fusion.3
  365.4 4.2 gather_fusion.2
  369.7 4.3 gather_fusion.1
  374.0 4.3 gather_fusion
  381.0 6.0 fusion.8
  387.9 13.9 %psum.28 = f32[1024]{0:T(1024)S(1)} all-reduce(f32[1024]{0:T(1024)S(1)} %get-tuple-element.35), channel_id=1, replica_groups=mesh['nodes'=96,'cols'=8] {'cols'}, use_global_device_ids=true, to_apply=%region_6.8 | all-reduce | flops 1024 | bytes 8192 | tf_op jit(solution)/shard_map/psum | solution.py:15
  402.2 11.2 %psum.29 = f32[1024]{0:T(1024)S(1)} all-reduce(f32[1024]{0:T(1024)S(1)} %fusion.11), channel_id=1, replica_groups=mesh['nodes'=96,'cols'=8] {'cols'}, use_global_device_ids=true, to_apply=%region_8.10 | all-reduce | flops 1024 | bytes 8192 | tf_op jit(solution)/shard_map/psum | solution.py:15
  414.6 81.9 %all_gather.7 = bf16[768,128]{1,0:T(8,128)(2,1)S(1)} all-gather(bf16[8,128]{1,0:T(8,128)(2,1)S(1)} %slice.101), channel_id=1, replica_groups=mesh['nodes'=96,'cols'=8] {'nodes'}, dimensions={0}, use_global_device_ids=true | all-gather | bytes 198656 | tf_op jit(solution)/shard_map/all_gather | solution.py:23
  496.5 1.6 mul.71
  498.1 25.5 %scatter_custom_fusion.2 = f32[768,128]{1,0:T(8,128)} fusion(s32[4096]{0:T(1024)S(1)} %reshape.95, f32[4096,128]{1,0:T(8,128)} %bitcast.35, f32[4096]{0:T(1024)S(1)} %reshape.105, f32[]{:T(128)} %constant.13.clone.1), kind=kCustom, calls=%fused_computation.20 | custom fusion | flops 1048576 | bytes 2506756 | tf_op jit(solution)/shard_map/scatter-add | solution.py:35
  524.9 256.0 %all-reduce.13.cloned.1.call-done = f32[768,128]{1,0:T(8,128)} async-done(((f32[768,128]{1,0:T(8,128)}), f32[768,128]{1,0:T(8,128)}) %all-reduce.13.cloned.1.call-update) | async-done | bytes 393232
  781.6 3.4 convolution_add_fusion
  785.0 44.4 %scatter_custom_fusion.3 = f32[1024,128]{1,0:T(8,128)S(1)} fusion(f32[1024,128]{1,0:T(8,128)S(1)} %convolution_add_fusion, s32[8192]{0:T(1024)S(1)} %reshape.119, f32[1024,128]{1,0:T(8,128)S(1)} %get-tuple-element.15), kind=kCustom, calls=%fused_computation.12 | custom fusion | flops 1048576 | bytes 1048576 | tf_op jit(solution)/shard_map/scatter-add | solution.py:79
  830.6 273.2 %all-reduce.15.cloned.1.call-done = (f32[1024,128]{0,1:T(8,128)}, f32[1024,128]{0,1:T(8,128)}) async-done(((f32[1024,128]{0,1:T(8,128)}, f32[1024,128]{0,1:T(8,128)}), (f32[1024,128]{0,1:T(8,128)}, f32[1024,128]{0,1:T(8,128)})) %all-reduce.15.cloned.1.call-update) | async-done | bytes 1048592 | tf_op jit(solution)/shard_map/psum | solution.py:83
  1103.9 2.0 copy.20
  1105.9 2.0 copy.21
  (62 shorter events, 13.3 us)
Async XLA Ops:
  7.2 2.7 copy-start
  7.2 2.7 copy-start.3
  7.2 373.2 %all-reduce.11.cloned.1.call-start = ((), (), s32[]{:S(2)}) async-start(), calls=%async_computation | async-start | bytes 786432
  10.6 56.0 %copy-start.6 = (s32[1024,4]{0,1:T(4,128)S(1)}, s32[1024,4]{0,1:T(4,128)}, u32[]{:S(2)}) copy-start(s32[1024,4]{0,1:T(4,128)} %param.14) | copy-start | bytes 49156
  10.6 56.0 %copy-start.5 = (s32[1024,4]{0,1:T(4,128)S(1)}, s32[1024,4]{0,1:T(4,128)}, u32[]{:S(2)}) copy-start(s32[1024,4]{0,1:T(4,128)} %param.13) | copy-start | bytes 49156
  10.6 56.0 %copy-start.4 = (s32[1024,8]{0,1:T(8,128)S(1)}, s32[1024,8]{0,1:T(8,128)}, u32[]{:S(2)}) copy-start(s32[1024,8]{0,1:T(8,128)} %param.12) | copy-start | bytes 98308
  37.7 743.3 %all-reduce.13.cloned.1.call-start = ((), (), s32[]{:S(2)}) async-start(), calls=%async_computation.1 | async-start | bytes 786432
  381.0 6.0 copy-start.7
  387.0 14.7 %copy-start.1 = (bf16[1024,128]{1,0:T(8,128)(2,1)S(1)}, bf16[1024,128]{1,0:T(8,128)(2,1)}, u32[]{:S(2)}) copy-start(bf16[1024,128]{1,0:T(8,128)(2,1)} %param.15) | copy-start | bytes 786436
  496.5 27.1 %copy-start.2 = (bf16[1024,128]{1,0:T(8,128)(2,1)S(1)}, bf16[1024,128]{1,0:T(8,128)(2,1)}, u32[]{:S(2)}) copy-start(bf16[1024,128]{1,0:T(8,128)(2,1)} %get-tuple-element.17) | copy-start | bytes 786436
  523.6 580.2 %all-reduce.15.cloned.1.call-start = ((), (), s32[]{:S(2)}) async-start(), calls=%async_computation.2 | async-start | bytes 2097152 | tf_op jit(solution)/shard_map/psum | solution.py:83
Sparse Core Ops, SparseCore 0:
  37.8 273.2 all-reduce.10
  523.7 257.1 all-reduce.12
  830.8 273.0 all-reduce.14
where the time goes:
time: 1120 us; the launch traced here: 1110 us
  waiting for transfers between devices  529 us (47%)
  blocking collectives  386 us (34%)
  other arithmetic  127 us (11%)
  local copies, waits for them, and re-layouts  44.3 us (4%)
  between operations  14.6 us (1%)
  matrix products  13.4 us (1%)
    psum x1, waiting for transfers between devices, local(): grad_self, grad_neigh = lax.psum((self_part, neigh_part), 'nodes')  273 us
    unnamed x5, waiting for transfers between devices  256 us
    unnamed x1, blocking collectives  196 us
    all_gather x2, blocking collectives, hub_parts(): piece = lax.all_gather(own_hubs, 'nodes', axis=0, tiled=True)  165 us
    scatter-add x2, other arithmetic, hub_parts(): jax.ops.segment_sum(spread, hub_link.reshape(-1), num_segments=total_hubs)  51 us
    scatter-add x1, other arithmetic, local(): jax.ops.segment_sum(repeated, local_nbr.reshape(-1), num_segments=row_count)  44.4 us
    gather x8, local copies, waits for them, and re-layouts, local(): jnp.take(proj_neigh, local_nbr[:, k], axis=0).astype(jnp.float32)  32.1 us
    scatter-add x1, other arithmetic, local(): jax.ops.segment_sum(used_mask.reshape(-1), hub_link.reshape(-1), num_segm...  28.8 us
  transfers between devices with their start and end apart: 3, of which 2 were waited for; matrix products, arithmetic and copies ran while one was open for 6% of the time, Pallas kernels for 0%

commit v1 on v0

v1 whole, which is shorter than its diff:
```python
import functools

import jax
import jax.numpy as jnp
from jax import lax
from jax.experimental import pallas as pl
from jax.experimental.pallas import tpu as pltpu
from jax.sharding import PartitionSpec as P

HUB_DEV = 8
FAN = 8
HFAN = 4
CORES = 2
GROUP_ROWS = 128
CHUNK = 256
EPSILON = 1e-05
X_CHIPS = 4

F32 = jnp.float32
BF16 = jnp.bfloat16
TALL = (((0,), (0,)), ((), ()))
WIDE = (((1,), (1,)), ((), ()))


def kernel(
    dims,
    feat,
    w_self,
    w_neigh,
    nbr,
    link,
    used,
    cot,
    out,
    grads,
    onehot,
    proj_self,
    proj_neigh,
    hub_rows,
    near,
    pre_act,
    push,
    push_in,
    zsend,
    zsend_in,
    own_p,

    own_sum,
    row_sums,
    low_grads,
    push2,
    push2_in,
    zsend2,
    zsend2_in,
    part,
    part_in,
    total,
    xsend,
    xsend_in,
    quarter,
    zq,
    zq_in,
    qfull,
    final,
    sems_z,
    sems_g,
    sems_y,
    sem_d,
    sems_x,
):
    xs, zs, ys = dims
    nodes, depth = feat.shape
    width = w_self.shape[1]
    hubs_z = zs * HUB_DEV
    groups = xs * CORES
    owners = 2 * zs // 3
    q_rows = depth // xs
    o_rows = q_rows // owners
    me = lax.axis_index("nodes")
    y = lax.axis_index("cols")
    c = lax.rem(me, CORES)
    z = lax.rem(me // CORES, zs)
    x = me // (CORES * zs)
    g = x * CORES + c

    def node(px, pz, pc):
        return (px * zs + pz) * CORES + pc

    def copy(src, dst, sems, row, slot, target):
        return pltpu.make_async_remote_copy(
            src_ref=src,
            dst_ref=dst,
            send_sem=sems.at[0, row, slot],
            recv_sem=sems.at[1, row, slot],
            device_id=target,
            device_id_type=pl.DeviceIdType.MESH,
        )

    def each(count, body):
        def step(k, carry):
            body(k)
            return carry

        lax.fori_loop(1, count, step, 0)

    def z_peer(k):
        pz = lax.rem(z + k, zs)
        return pz, (node(x, pz, c), y)

    def g_peer(k):
        px = lax.rem(x + k // CORES, xs)
        pc = lax.rem(c + lax.rem(k, CORES), CORES)
        return px * CORES + pc, (node(px, z, pc), y)

    def y_peer(k):
        return me, lax.rem(y + k, ys)

    def x_peer(k):
        px = lax.rem(x + k, xs)
        return px, (node(px, z, c), y)

    partner = (node(x, z, 1 - c), y)

    hub_rows[...] = jnp.zeros_like(hub_rows)
    barrier = pltpu.get_barrier_semaphore()

    def greet(target):
        pl.semaphore_signal(barrier, inc=1, device_id=target, device_id_type=pl.DeviceIdType.MESH)

    each(zs, lambda k: greet(z_peer(k)[1]))
    each(groups, lambda k: greet(g_peer(k)[1]))
    each(ys, lambda k: greet(y_peer(k)))

    own_p[z] = jnp.dot(feat[0:16, :], w_neigh[...], preferred_element_type=F32)[0:HUB_DEV]

    hub = link[...]
    place = hub % HUB_DEV
    device = hub // HUB_DEV
    core = device % CORES
    chip = device // CORES
    hub_x = jnp.zeros_like(chip)
    for i in range(1, xs):
        hub_x = hub_x + (chip >= i * zs).astype(jnp.int32)
    hub_z = chip - hub_x * zs
    column = (hub_x * CORES + core) * GROUP_ROWS + hub_z * HUB_DEV + place
    column = jnp.where(used[...] > 0, column, -1)
    link_base = nodes

    def build(first, count, picks, base):
        tile = 32

        def step(i, carry):
            row = i * tile
            ids = lax.broadcasted_iota(jnp.int32, (tile, nodes), 0) + row
            acc = jnp.zeros((tile, nodes), F32)
            for k in range(picks.shape[0]):
                acc = acc + jnp.where(ids == picks[k : k + 1, :], 1.0, 0.0)
            onehot[pl.ds(pl.multiple_of(base + row, tile), tile), :] = acc.astype(BF16)
            return carry

        lax.fori_loop(0, count // tile, step, 0)

    link_cols = groups * GROUP_ROWS
    build(0, link_cols, column, link_base)

    node_ones = jnp.ones((HUB_DEV, nodes), BF16)
    slice_cols = pl.ds(pl.multiple_of(y * width, 128), width)

    def push_step(i, carry):
        rows = onehot[pl.ds(pl.multiple_of(link_base + i * GROUP_ROWS, GROUP_ROWS), GROUP_ROWS), :]
        push[i] = jnp.dot(rows, feat[:, slice_cols], preferred_element_type=F32)
        push[i, hubs_z : hubs_z + HUB_DEV, 0:GROUP_ROWS] = lax.dot_general(
            node_ones, rows, WIDE, preferred_element_type=F32
        )
        return carry

    lax.fori_loop(0, groups, push_step, 0)

    pl.semaphore_wait(barrier, zs + groups + ys - 3)

    ap_z = lambda k: copy(own_p.at[z], own_p.at[z], sems_z, 0, k - 1, z_peer(k)[1])

    def pushx(k):
        pg, target = g_peer(k)
        return copy(
            push.at[pg, pl.ds(0, hubs_z + HUB_DEV)], push_in.at[k - 1], sems_g, 0, k - 1, target
        )

    each(zs, lambda k: ap_z(k).start())
    each(groups, lambda k: pushx(k).start())

    def proj_step(i, carry):
        rows = pl.ds(pl.multiple_of(i * CHUNK, CHUNK), CHUNK)
        both = jnp.dot(
            feat[rows, :],
            jnp.concatenate([w_self[...], w_neigh[...]], axis=1),
            preferred_element_type=F32,
        )
        proj_self[rows, :] = both[:, :width]
        proj_neigh[rows, :] = both[:, width:].astype(BF16)
        return carry

    lax.fori_loop(0, nodes // CHUNK, proj_step, 0)

    each(zs, lambda k: ap_z(k).wait())
    plane_rows = own_p[...].reshape(hubs_z, width).astype(BF16)
    hub_rows[g, 0:hubs_z] = plane_rows

    def ap_x(k):
        pg, target = g_peer(k)
        mine = hub_rows.at[g, pl.ds(0, hubs_z)]
        return copy(mine, mine, sems_g, 1, k - 1, target)

    each(groups, lambda k: ap_x(k).start())

    each(groups, lambda k: pushx(k).wait())
    summed = push[g, 0 : hubs_z + HUB_DEV]
    for k in range(groups - 1):
        summed = summed + push_in[k]
    for i in range(zs):
        zsend[i, 0:HUB_DEV] = summed[i * HUB_DEV : (i + 1) * HUB_DEV]
        zsend[i, HUB_DEV : 2 * HUB_DEV] = summed[hubs_z : hubs_z + HUB_DEV]

    def pushz(k):
        pz, target = z_peer(k)
        return copy(zsend.at[pz], zsend_in.at[k - 1], sems_z, 1, k - 1, target)

    each(zs, lambda k: pushz(k).start())

    build(0, nodes, nbr[...], 0)

    def near_step(i, carry):
        cols = pl.ds(pl.multiple_of(i * CHUNK, CHUNK), CHUNK)
        near[cols, :] = lax.dot_general(
            onehot[0:nodes, cols], proj_neigh[...], TALL, preferred_element_type=F32
        )
        return carry

    lax.fori_loop(0, nodes // CHUNK, near_step, 0)

    each(zs, lambda k: pushz(k).wait())
    hub_sum = zsend[z]
    for k in range(zs - 1):
        hub_sum = hub_sum + zsend_in[k]
    own_sum[y] = hub_sum[0:HUB_DEV]
    count_block = hub_sum[HUB_DEV : 2 * HUB_DEV]
    lane = lax.broadcasted_iota(jnp.int32, count_block.shape, 1)
    sub = lax.broadcasted_iota(jnp.int32, count_block.shape, 0)
    count_in = jnp.sum(
        jnp.where(lane == sub + z * HUB_DEV, count_block, 0.0), axis=1, keepdims=True
    )
    sum_y = lambda k: copy(own_sum.at[y], own_sum.at[y], sems_y, 0, k - 1, y_peer(k))
    each(ys, lambda k: sum_y(k).start())

    each(groups, lambda k: ap_x(k).wait())
    pulled_rhs = jnp.concatenate(
        [hub_rows[...].reshape(link_cols, width), jnp.ones((link_cols, width), BF16)], axis=1
    )

    def pull_step(i, carry):
        cols = pl.ds(pl.multiple_of(i * CHUNK, CHUNK), CHUNK)
        both = lax.dot_general(
            onehot[pl.ds(link_base, link_cols), cols],
            pulled_rhs,
            TALL,
            preferred_element_type=F32,
        )
        near[cols, :] = near[cols, :] + both[:, :width]
        pre_act[cols, :] = FAN + both[:, width:]
        return carry

    lax.fori_loop(0, nodes // CHUNK, pull_step, 0)

    each(ys, lambda k: sum_y(k).wait())
    linked = jnp.concatenate([own_sum[i] for i in range(ys)], axis=1)
    linked_high = linked.astype(BF16).astype(F32)
    linked_low = linked - linked_high
    inflow = jnp.dot(
        jnp.concatenate([linked_high, linked_low], axis=0).astype(BF16),
        w_neigh[...],
        preferred_element_type=F32,
    )
    near[0:HUB_DEV, :] = near[0:HUB_DEV, :] + (inflow[0:HUB_DEV] + inflow[HUB_DEV:])
    pre_act[0:HUB_DEV, :] = pre_act[0:HUB_DEV, :] + count_in

    chunks = nodes // CHUNK
    lanes = lax.broadcasted_iota(jnp.int32, (2 * chunks, width), 0)
    sums = jnp.zeros((2 * chunks, CHUNK), F32)
    for i in range(chunks):
        rows = slice(i * CHUNK, (i + 1) * CHUNK)
        degree = pre_act[rows, :]
        pre = proj_self[rows, :] + near[rows, :] / degree
        act = pre * jax.nn.sigmoid(pre)
        near[rows, :] = degree
        pre_act[rows, :] = pre
        for at, value in ((i, act * act), (chunks + i, act * cot[rows, :].astype(F32))):
            sums = sums + lax.dot_general(
                jnp.where(lanes == at, 1.0, 0.0),
                value,
                WIDE,
                preferred_element_type=F32,
                precision=lax.Precision.HIGHEST,
            )
    row_sums[y] = sums
    sum_c = lambda k: copy(row_sums.at[y], row_sums.at[y], sems_y, 1, k - 1, y_peer(k))
    each(ys, lambda k: sum_c(k).start())
    each(ys, lambda k: sum_c(k).wait())
    sums = row_sums[0]
    for i in range(1, ys):
        sums = sums + row_sums[i]
    inv_scale = 1.0 / jnp.sqrt(sums[0:chunks] / depth + EPSILON)
    inner = sums[chunks:] * inv_scale / depth
    by_row = jnp.transpose(jnp.concatenate([inv_scale, inner], axis=0))

    for i in range(chunks):
        rows = slice(i * CHUNK, (i + 1) * CHUNK)
        pre = pre_act[rows, :]
        sig = jax.nn.sigmoid(pre)
        inv = by_row[:, i : i + 1]
        normed = pre * sig * inv
        out[rows, :] = normed.astype(BF16)
        slope = sig * (1.0 + pre * (1.0 - sig))
        grad = (cot[rows, :].astype(F32) - normed * by_row[:, chunks + i : chunks + i + 1]) * inv * slope
        low_grads[rows, 0:width] = grad.astype(BF16)
        low_grads[rows, width:] = (grad / near[rows, :]).astype(BF16)

    def push2_step(i, carry):
        push2[i] = jnp.dot(
            onehot[pl.ds(pl.multiple_of(link_base + i * GROUP_ROWS, GROUP_ROWS), GROUP_ROWS), :],
            low_grads[:, width:],
            preferred_element_type=F32,
        )
        return carry

    lax.fori_loop(0, groups, push2_step, 0)

    def push2x(k):
        pg, target = g_peer(k)
        return copy(push2.at[pg, pl.ds(0, hubs_z)], push2_in.at[k - 1], sems_g, 2, k - 1, target)

    each(groups, lambda k: push2x(k).start())
    own_scaled = low_grads[0:16, width:].astype(F32)[0:HUB_DEV]

    def part_step(which):
        def step(i, carry):
            cols = pl.ds(pl.multiple_of(i * CHUNK, CHUNK), CHUNK)
            part[which, cols, :] = lax.dot_general(
                feat[:, cols],
                low_grads[:, which * width : (which + 1) * width],
                TALL,
                preferred_element_type=F32,
            )
            return carry

        lax.fori_loop(0, depth // CHUNK, step, 0)

    part_step(0)
    swap = pltpu.make_async_remote_copy(
        src_ref=part.at[1 - c],
        dst_ref=part_in,
        send_sem=sem_d.at[0],
        recv_sem=sem_d.at[1],
        device_id=partner,
        device_id_type=pl.DeviceIdType.MESH,
    )

    @pl.when(c == 1)
    def _():
        swap.start()

    def back_step(i, carry):
        rows = pl.ds(pl.multiple_of(i * CHUNK, CHUNK), CHUNK)
        near[rows, :] = jnp.dot(onehot[rows, :], low_grads[:, width:], preferred_element_type=F32)
        return carry

    lax.fori_loop(0, nodes // CHUNK, back_step, 0)

    each(groups, lambda k: push2x(k).wait())
    summed = push2[g, 0:hubs_z]
    for k in range(groups - 1):
        summed = summed + push2_in[k]
    zsend2[...] = summed.reshape(zs, HUB_DEV, width)

    def push2z(k):
        pz, target = z_peer(k)
        return copy(zsend2.at[pz], zsend2_in.at[k - 1], sems_z, 2, k - 1, target)

    each(zs, lambda k: push2z(k).start())

    low_grads[:, width:] = near[...].astype(BF16)
    part_step(1)

    def sendx(k):
        px, target = x_peer(k)
        return copy(xsend.at[px], xsend_in.at[k - 1], sems_x, 0, k - 1, target)

    def open_x():
        swap.wait_recv()
        for i in range(xs):
            rows = slice(i * q_rows, (i + 1) * q_rows)
            both = part[c, rows, :] + part_in[rows, :]
            total[i] = both
            xsend[i] = both.astype(BF16)
        each(xs, lambda k: sendx(k).start())

    @pl.when(c == 0)
    def _():
        open_x()

    each(zs, lambda k: push2z(k).wait())
    back = zsend2[z]
    for k in range(zs - 1):
        back = back + zsend2_in[k]
    back_high = back.astype(BF16).astype(F32)
    own_feat = feat[0:16, :].astype(F32)[0:HUB_DEV]
    tall = jnp.concatenate([own_feat, own_feat, linked_high, linked_low], axis=0).astype(BF16)
    flat = jnp.concatenate([back_high, back - back_high, own_scaled, own_scaled], axis=0).astype(BF16)
    part[1] = part[1] + lax.dot_general(tall, flat, TALL, preferred_element_type=F32)

    @pl.when(c == 0)
    def _():
        swap.start()

    @pl.when(c == 1)
    def _():
        open_x()

    each(xs, lambda k: sendx(k).wait())
    reduced = total[x]
    for k in range(xs - 1):
        reduced = reduced + xsend_in[k].astype(F32)
    quarter[...] = reduced.reshape(owners, o_rows, width)
    zq[...] = reduced.astype(BF16).reshape(owners, o_rows, width)

    def owns(pz):
        return lax.rem(pz, 3) != 2

    def rank(pz):
        return (pz // 3) * 2 + lax.rem(pz, 3)

    def sendq(k):
        pz, target = z_peer(k)
        return copy(zq.at[rank(pz)], zq_in.at[k - 1], sems_z, 3, k - 1, target)

    def start_q(k):
        @pl.when(owns(z_peer(k)[0]))
        def _():
            sendq(k).start()

    each(zs, start_q)

    def sendf(k):
        _, target = z_peer(k)
        mine = qfull.at[rank(z)]
        return copy(mine, mine, sems_z, 4, k - 1, target)

    waitq = lambda k: copy(zq.at[0], zq_in.at[k - 1], sems_z, 3, k - 1, z_peer(k)[1])
    waitf = lambda k: copy(qfull.at[0], qfull.at[0], sems_z, 4, k - 1, z_peer(k)[1])

    @pl.when(owns(z))
    def _():
        each(zs, lambda k: waitq(k).wait_recv())
        mine = quarter[rank(z)]
        for k in range(zs - 1):
            mine = mine + zq_in[k].astype(F32)
        qfull[rank(z)] = mine.astype(BF16)
        each(zs, lambda k: sendf(k).start())

    def finish_q(k):
        @pl.when(owns(z_peer(k)[0]))
        def _():
            waitq(k).wait_send()

        @pl.when(owns(lax.rem(z + zs - k, zs)))
        def _():
            waitf(k).wait_recv()

    each(zs, finish_q)
    final[c, x] = qfull[...].reshape(q_rows, width)

    def sendq_x(k):
        _, target = x_peer(k)
        mine = final.at[c, x]
        return copy(mine, mine, sems_x, 1, k - 1, target)

    def forward(k):
        px = lax.rem(x + xs - k, xs)
        piece = final.at[c, px]
        return copy(piece, piece, sems_x, 2, k, partner)

    each(xs, lambda k: sendq_x(k).start())
    forward(0).start()

    def pass_on(k):
        sendq_x(k).wait_recv()
        forward(k).start()

    each(xs, pass_on)
    forward(0).wait()
    each(xs, lambda k: forward(k).wait())
    each(xs, lambda k: sendq_x(k).wait_send())
    swap.wait_send()

    @pl.when(owns(z))
    def _():
        each(zs, lambda k: waitf(k).wait_send())

    grads[...] = final[...].reshape(CORES, depth, width)


def local(dims, features, w_self, w_neigh, local_nbr, hub_link, hub_used, cotangent):
    xs, zs, ys = dims
    nodes, depth = features.shape
    width = w_self.shape[1]
    groups = xs * CORES
    hubs_z = zs * HUB_DEV
    owners = 2 * zs // 3
    q_rows = depth // xs
    o_rows = q_rows // owners
    link_cols = groups * GROUP_ROWS
    vmem = pltpu.VMEM
    scratch = [
        vmem((nodes + link_cols, nodes), BF16),
        vmem((nodes, width), F32),
        vmem((nodes, width), BF16),
        vmem((groups, GROUP_ROWS, width), BF16),
        vmem((nodes, width), F32),
        vmem((nodes, width), F32),
        vmem((groups, GROUP_ROWS, width), F32),
        vmem((groups - 1, hubs_z + HUB_DEV, width), F32),
        vmem((zs, 2 * HUB_DEV, width), F32),
        vmem((zs - 1, 2 * HUB_DEV, width), F32),
        vmem((zs, HUB_DEV, width), F32),

        vmem((ys, HUB_DEV, width), F32),
        vmem((ys, 2 * (nodes // CHUNK), CHUNK), F32),
        vmem((nodes, 2 * width), BF16),
        vmem((groups, GROUP_ROWS, width), F32),
        vmem((groups - 1, hubs_z, width), F32),
        vmem((zs, HUB_DEV, width), F32),
        vmem((zs - 1, HUB_DEV, width), F32),
        vmem((CORES, depth, width), F32),
        vmem((depth, width), F32),
        vmem((xs, q_rows, width), F32),
        vmem((xs, q_rows, width), BF16),
        vmem((xs - 1, q_rows, width), BF16),
        vmem((owners, o_rows, width), F32),
        vmem((owners, o_rows, width), BF16),
        vmem((zs - 1, o_rows, width), BF16),
        vmem((owners, o_rows, width), BF16),
        vmem((CORES, xs, q_rows, width), BF16),
        pltpu.SemaphoreType.DMA((2, 5, zs - 1)),
        pltpu.SemaphoreType.DMA((2, 3, groups - 1)),
        pltpu.SemaphoreType.DMA((2, 2, ys - 1)),
        pltpu.SemaphoreType.DMA((2,)),
        pltpu.SemaphoreType.DMA((2, 3, xs)),
    ]
    whole = pl.BlockSpec(memory_space=pltpu.VMEM)
    output, grads = pl.pallas_call(
        functools.partial(kernel, dims),
        out_shape=(
            jax.ShapeDtypeStruct((nodes, width), BF16),
            jax.ShapeDtypeStruct((CORES, depth, width), BF16),
        ),
        in_specs=[whole] * 7,
        out_specs=(whole, whole),
        scratch_shapes=scratch,
        compiler_params=pltpu.CompilerParams(
            collective_id=0, has_side_effects=True, vmem_limit_bytes=56 * 1024 * 1024
        ),
    )(features, w_self, w_neigh, local_nbr.T, hub_link.T, hub_used.T, cotangent)
    return output, grads[0].astype(F32), grads[1].astype(F32)


def solution(mesh):
    ys = mesh.shape["cols"]
    xs = X_CHIPS
    zs = mesh.shape["nodes"] // (xs * CORES)
    placed = (
        P("nodes", None),
        P(None, "cols"),
        P(None, "cols"),
        P("nodes", None),
        P("nodes", None),
        P("nodes", None),
        P("nodes", "cols"),
    )
    return jax.shard_map(
        functools.partial(local, (xs, zs, ys)),
        mesh=mesh,
        in_specs=placed,
        out_specs=(P("nodes", "cols"), P(None, "cols"), P(None, "cols")),
        check_vma=False,
    )
```

time: 1120 us -> 90 us (0.08)
  waiting for transfers between devices: 529 us -> 0 us
  blocking collectives: 386 us -> 0 us
  other arithmetic: 127 us -> 2.07 us
  Pallas kernels: 0 us -> 85.4 us
  local copies, waits for them, and re-layouts: 44.3 us -> 1.67 us
  between operations: 14.6 us -> 0.64 us
  matrix products: 13.4 us -> 0 us
    psum x1 -> x0, waiting for transfers between devices: 273 us -> none  [local(): grad_self, grad_neigh = lax.psum((self_part, neigh_part), 'nodes')]
    unnamed x5 -> x0, waiting for transfers between devices: 256 us -> none
    unnamed x1 -> x0, blocking collectives: 196 us -> none
    all_gather x2 -> x0, blocking collectives: 165 us -> none  [hub_parts(): piece = lax.all_gather(own_hubs, 'nodes', axis=0, tiled=True)]
    scatter-add x4 -> x0, other arithmetic: 124 us -> none  [the longest x2 51 us: hub_parts(): jax.ops.segment_sum(spread, hub_link.reshape(-1), num_segments=total_hubs)]
    pallas_call x0 -> x1, Pallas kernels: none -> 85.4 us  [local(): pl.pallas_call(functools.partial(kernel, dims), out_shape=(jax.ShapeDtype...]
    gather x8 -> x0, local copies, waits for them, and re-layouts: 32.1 us -> none  [local(): jnp.take(proj_neigh, local_nbr[:, k], axis=0).astype(jnp.float32)]
    psum x2 -> x0, blocking collectives: 25.1 us -> none  [column_total(): return lax.psum(values, 'cols')]
  transfers between devices with their start and end apart: 3 -> 0, of which waited for: 2 -> 0; matrix products, arithmetic and copies ran while one was open for 6% -> 0% of each run, Pallas kernels for 0% -> 0%
where the time goes in v1:
time: 90 us; the launch traced here: 89.8 us
  Pallas kernels  85.4 us (95%)
  other arithmetic  2.07 us (2%)
  local copies, waits for them, and re-layouts  1.67 us (2%)
    pallas_call x1, Pallas kernels, local(): pl.pallas_call(functools.partial(kernel, dims), out_shape=(jax.ShapeDtype...  85.4 us
    convert_element_type x1, other arithmetic, local(): return (output, grads[0].astype(F32), grads[1].astype(F32))  2.07 us

profile of v1, /device:TPU:1, one launch (start us, length us, event | category | flops | bytes accessed | tf_op | source)
XLA Modules:
  0.0 89.8 jit_solution(7142664671699289709)
XLA Ops:
  0.6 85.4 %shard_map.94 = (bf16[1024,128]{1,0:T(8,128)(2,1)}, bf16[2,1024,128]{2,1,0:T(8,128)(2,1)}) custom-call(bf16[1024,1024]{1,0:T(8,128)(2,1)} %feat.1, bf16[1024,128]{1,0:T(8,128)(2,1)} %w_self.1, bf16[1024,128]{1,0:T(8,128)(2,1)} %w_neigh.1, s32[8,1024]{1,0:T(8,128)} %bitcast.9, s32[4,1024]{1,0:T(4,128)} %bitcast.10, s32[4,1024]{1,0:T(4,128)} %bitcast.11, ...), custom_call_target="tpu_custom_call" | custom-call | tf_op jit(solution)/shard_map/pallas_call | solution.py:559
  86.1 2.1 %bitcast_convert_fusion = (f32[1024,128]{1,0:T(8,128)}, f32[1024,128]{1,0:T(8,128)}) fusion(bf16[2,1024,128]{2,1,0:T(8,128)(2,1)} %get-tuple-element.6), kind=kLoop, calls=%fused_computation | loop fusion | flops 262144 | bytes 1572864 | tf_op jit(solution)/shard_map/convert_element_type | solution.py:572
  88.1 1.7 %copy.11 = bf16[1024,128]{1,0:T(8,128)(2,1)} copy(bf16[1024,128]{1,0:T(8,128)(2,1)} %get-tuple-element.12) | data formatting | bytes 524288

commit v2 on v0

v2 whole, which is shorter than its diff:
```python
import functools
import types

import jax
import jax.numpy as jnp
from jax import lax
from jax.experimental import pallas as pl
from jax.experimental.pallas import tpu as pltpu
from jax.sharding import PartitionSpec as P

HUB_DEV = 8
FAN = 8
CORES = 2
GROUP_ROWS = 128
CHUNK = 256
TILE = 32
EPSILON = 1e-05
X_CHIPS = 4

F32 = jnp.float32
BF16 = jnp.bfloat16
TALL = (((0,), (0,)), ((), ()))
WIDE = (((1,), (1,)), ((), ()))


def sizes(dims, nodes, depth, width):
    xs, zs, ys = dims
    s = types.SimpleNamespace(xs=xs, zs=zs, ys=ys, nodes=nodes, depth=depth, width=width)
    s.groups = xs * CORES
    s.hubs_z = zs * HUB_DEV
    s.owners = 2 * zs // 3
    s.q_rows = depth // xs
    s.o_rows = s.q_rows // s.owners
    s.link_cols = s.groups * GROUP_ROWS
    s.chunks = nodes // CHUNK
    return s


def scratch_of(s):
    vmem = pltpu.VMEM
    dma = pltpu.SemaphoreType.DMA
    w = s.width
    sum_rows = 2 * s.chunks
    hub_k = 2 * s.hubs_z + 2 * HUB_DEV
    return {
        "feat": vmem((s.nodes, s.depth), BF16),
        "w_self": vmem((s.depth, w), BF16),
        "w_neigh": vmem((s.depth, w), BF16),
        "nbr": vmem((FAN, s.nodes), jnp.int32),
        "link": vmem((4, s.nodes), jnp.int32),
        "used": vmem((4, s.nodes), jnp.int32),
        "cot": vmem((s.nodes, w), BF16),
        "links": vmem((s.link_cols, s.nodes), BF16),
        "locals_": vmem((s.nodes, s.nodes), BF16),
        "proj_self": vmem((s.nodes, w), F32),
        "pushable": vmem((s.nodes, 2 * w), BF16),
        "hub_rows": vmem((s.groups, GROUP_ROWS, w), BF16),
        "near": vmem((s.nodes, w), F32),
        "degree": vmem((s.nodes, w), F32),
        "pre_act": vmem((s.nodes, w), F32),
        "push": vmem((s.groups, s.hubs_z, 2 * w), F32),
        "push_p": vmem((s.groups, s.hubs_z + 16, w), BF16),
        "push_p_in": vmem((s.groups - 1, s.hubs_z + 16, w), BF16),
        "push_g": vmem((s.groups, s.hubs_z, w), BF16),
        "push_g_in": vmem((s.groups - 1, s.hubs_z, w), BF16),
        "zsend_p": vmem((s.zs, 2 * HUB_DEV, w), F32),
        "zsend_p_in": vmem((s.zs - 1, 2 * HUB_DEV, w), F32),
        "zsend_g": vmem((s.zs, HUB_DEV, w), F32),
        "zsend_g_in": vmem((s.zs - 1, HUB_DEV, w), F32),
        "own_p": vmem((s.zs, HUB_DEV, w), F32),
        "own_sum": vmem((s.ys, HUB_DEV, w), F32),
        "hub_feat": vmem((s.zs, 2 * HUB_DEV, s.depth // 2), BF16),
        "sums_a": vmem((s.ys, sum_rows, CHUNK), F32),
        "sums_b": vmem((s.ys, sum_rows, CHUNK), F32),
        "low": vmem((s.nodes, w), BF16),
        "scaled": vmem((s.nodes, w), BF16),
        "back": vmem((s.nodes, w), F32),
        "back_low": vmem((s.nodes, w), BF16),
        "push2": vmem((s.groups, GROUP_ROWS, w), F32),
        "push2_low": vmem((s.groups, s.hubs_z, w), BF16),
        "push2_in": vmem((s.groups - 1, s.hubs_z, w), BF16),
        "tall": vmem((hub_k, s.depth), BF16),
        "part": vmem((CORES, s.xs, s.q_rows, w), F32),
        "part_in": vmem((s.xs, s.q_rows, w), F32),
        "total": vmem((s.q_rows, w), F32),
        "xsend": vmem((s.xs, s.q_rows, w), BF16),
        "xsend_in": vmem((s.xs - 1, s.q_rows, w), BF16),
        "quarter": vmem((s.owners, s.o_rows, w), F32),
        "zq": vmem((s.owners, s.o_rows, w), BF16),
        "zq_in": vmem((s.zs - 1, s.o_rows, w), BF16),
        "final": vmem((CORES, s.xs, s.owners, s.o_rows, w), BF16),
        "sems_z": dma((2, 6, s.zs - 1)),
        "sems_g": dma((2, 4, s.groups - 1)),
        "sems_y": dma((2, 3, s.ys - 1)),
        "sems_x": dma((2, 3, s.xs)),
        "sems_f": dma((2, s.xs - 1, s.owners)),
        "sems_l": dma((7,)),
    }


def kernel(s, names, feat_in, w_self_in, w_neigh_in, nbr_in, link_in, used_in, cot_in, out, grads, *refs):
    r = types.SimpleNamespace(**dict(zip(names, refs)))
    xs, zs, ys, width, nodes = s.xs, s.zs, s.ys, s.width, s.nodes
    groups, hubs_z, owners, q_rows = s.groups, s.hubs_z, s.owners, s.q_rows
    chunks = s.chunks
    me = lax.axis_index("nodes")
    y = lax.axis_index("cols")
    c = lax.rem(me, CORES)
    z = lax.rem(me // CORES, zs)
    x = me // (CORES * zs)
    g = x * CORES + c

    def node(px, pz, pc):
        return (px * zs + pz) * CORES + pc

    def copy(src, dst, sems, row, slot, target):
        return pltpu.make_async_remote_copy(
            src_ref=src,
            dst_ref=dst,
            send_sem=sems.at[0, row, slot],
            recv_sem=sems.at[1, row, slot],
            device_id=target,
            device_id_type=pl.DeviceIdType.MESH,
        )

    def loop(count, body):
        def step(i, carry):
            body(i)
            return carry

        lax.fori_loop(0, count, step, 0)

    def ranked(count, i):
        return count // 2 + (i // 2) * (1 - 2 * lax.rem(i, 2))

    def each(count, body):
        loop(count - 1, lambda i: body(ranked(count, i + 1)))

    def each_near(count, body):
        loop(count - 1, lambda i: body(ranked(count, count - 1 - i)))

    def z_peer(k):
        pz = lax.rem(z + k, zs)
        return pz, (node(x, pz, c), y)

    def g_peer(k):
        px = lax.rem(x + k // CORES, xs)
        pc = lax.rem(c + lax.rem(k, CORES), CORES)
        return px * CORES + pc, (node(px, z, pc), y)

    def y_peer(k):
        return me, lax.rem(y + k, ys)

    def x_peer(k):
        px = lax.rem(x + k, xs)
        return px, (node(px, z, c), y)

    partner = (node(x, z, 1 - c), y)

    barrier = pltpu.get_barrier_semaphore()

    def greet(target):
        pl.semaphore_signal(barrier, inc=1, device_id=target, device_id_type=pl.DeviceIdType.MESH)

    each(zs, lambda k: greet(z_peer(k)[1]))
    each(ys, lambda k: greet(y_peer(k)))
    each(groups, lambda k: greet(g_peer(k)[1]))
    inputs = [
        pltpu.make_async_copy(src, dst, r.sems_l.at[i])
        for i, (src, dst) in enumerate(
            (
                (link_in, r.link),
                (used_in, r.used),
                (w_neigh_in, r.w_neigh),
                (feat_in, r.feat),
                (w_self_in, r.w_self),
                (nbr_in, r.nbr),
                (cot_in, r.cot),
            )
        )
    ]
    for item in inputs:
        item.start()
    r.hub_rows[:, hubs_z:] = jnp.zeros((groups, GROUP_ROWS - hubs_z, width), BF16)

    def build(dest, base, count, picks):
        for first in range(0, count, TILE):
            ids = lax.broadcasted_iota(jnp.int32, (TILE, nodes), 0) + (base + first)
            acc = jnp.zeros((TILE, nodes), F32)
            for k in range(picks.shape[0]):
                acc = acc + jnp.where(ids == picks[k : k + 1, :], 1.0, 0.0)
            dest[pl.ds(pl.multiple_of(base + first, TILE), TILE), :] = acc.astype(BF16)

    inputs[0].wait()
    inputs[1].wait()
    hub = r.link[...]
    place = lax.rem(hub, HUB_DEV)
    device = lax.div(hub, HUB_DEV)
    core = lax.rem(device, CORES)
    chip = lax.div(device, CORES)
    hub_x = jnp.zeros_like(chip)
    for i in range(1, xs):
        hub_x = hub_x + (chip >= i * zs).astype(jnp.int32)
    hub_z = chip - hub_x * zs
    column = (hub_x * CORES + core) * GROUP_ROWS + hub_z * HUB_DEV + place
    r.link[...] = jnp.where(r.used[...] > 0, column, -1)
    tiles = -(-hubs_z // TILE) * TILE

    def build_links(i):
        base = i * GROUP_ROWS
        build(r.links, base, tiles, r.link[...])
        if tiles < GROUP_ROWS:
            rest = GROUP_ROWS - tiles
            r.links[pl.ds(pl.multiple_of(base + tiles, TILE), rest), :] = jnp.zeros((rest, nodes), BF16)

    loop(groups, build_links)

    inputs[2].wait()
    inputs[3].wait()
    own_rows = r.feat[0:16, :]
    r.own_p[z] = jnp.dot(own_rows, r.w_neigh[...], preferred_element_type=F32)[0:HUB_DEV]
    pl.semaphore_wait(barrier, zs + groups + ys - 3)

    def gather_z(k):
        mine = r.own_p.at[z]
        return copy(mine, mine, r.sems_z, 0, k - 1, z_peer(k)[1])

    each(zs, lambda k: gather_z(k).start())

    def proj_step(i):
        rows = pl.ds(pl.multiple_of(i * CHUNK, CHUNK), CHUNK)
        r.pushable[rows, 0:width] = jnp.dot(
            r.feat[rows, :], r.w_neigh[...], preferred_element_type=F32
        ).astype(BF16)
        r.pushable[rows, width:] = r.feat[rows, pl.ds(pl.multiple_of(y * width, 128), width)]

    loop(chunks, proj_step)
    node_ones = jnp.ones((HUB_DEV, nodes), BF16)

    def push_p(pg, k):
        target = g_peer(k)[1]
        return copy(r.push_p.at[pg], r.push_p_in.at[k - 1], r.sems_g, 0, k - 1, target)

    def push_g(pg, k):
        target = g_peer(k)[1]
        return copy(r.push_g.at[pg], r.push_g_in.at[k - 1], r.sems_g, 1, k - 1, target)

    def push_rows(pg):
        rows = r.links[pl.ds(pl.multiple_of(pg * GROUP_ROWS, GROUP_ROWS), GROUP_ROWS), :]
        both = jnp.dot(rows, r.pushable[...], preferred_element_type=F32)[0:hubs_z]
        count = lax.dot_general(node_ones, rows, WIDE, preferred_element_type=F32)
        count_high = count.astype(BF16).astype(F32)
        counts = jnp.concatenate([count_high, count - count_high], axis=0)
        r.push[pg] = both
        r.push_p[pg, 0:hubs_z] = both[:, :width].astype(BF16)
        r.push_p[pg, hubs_z:] = counts.astype(BF16)
        r.push_g[pg] = both[:, width:].astype(BF16)

    def push_to(k):
        pg = g_peer(k)[0]
        push_rows(pg)
        push_p(pg, k).start()

    each(groups, push_to)
    push_rows(g)
    each(groups, lambda k: push_g(g_peer(k)[0], k).start())

    each(zs, lambda k: gather_z(k).wait())
    r.hub_rows[g, 0:hubs_z] = r.own_p[...].reshape(hubs_z, width).astype(BF16)

    def gather_g(k):
        mine = r.hub_rows.at[g, pl.ds(0, hubs_z)]
        return copy(mine, mine, r.sems_g, 2, k - 1, g_peer(k)[1])

    each(groups, lambda k: gather_g(k).start())

    inputs[5].wait()
    loop(nodes // 128, lambda i: build(r.locals_, i * 128, 128, r.nbr[...]))

    each(groups, lambda k: push_p(g_peer(k)[0], k).wait())
    summed = r.push[g, :, 0:width]
    counts = r.push_p[g, hubs_z:].astype(F32)
    for k in range(groups - 1):
        summed = summed + r.push_p_in[k, 0:hubs_z].astype(F32)
        counts = counts + r.push_p_in[k, hubs_z:].astype(F32)
    counts = counts[0:HUB_DEV] + counts[HUB_DEV:]
    for i in range(zs):
        r.zsend_p[i, 0:HUB_DEV] = summed[i * HUB_DEV : (i + 1) * HUB_DEV]
        r.zsend_p[i, HUB_DEV:] = counts

    def push_pz(k):
        pz, target = z_peer(k)
        return copy(r.zsend_p.at[pz], r.zsend_p_in.at[k - 1], r.sems_z, 1, k - 1, target)

    each(zs, lambda k: push_pz(k).start())

    inputs[4].wait()

    def near_step(i):
        rows = pl.ds(pl.multiple_of(i * CHUNK, CHUNK), CHUNK)
        r.proj_self[rows, :] = jnp.dot(r.feat[rows, :], r.w_self[...], preferred_element_type=F32)
        r.near[rows, :] = lax.dot_general(
            r.locals_[:, rows], r.pushable[:, 0:width], TALL, preferred_element_type=F32
        )

    loop(chunks, near_step)

    each(groups, lambda k: gather_g(k).wait())

    def pull_step(i):
        cols = pl.ds(pl.multiple_of(i * CHUNK, CHUNK), CHUNK)
        pulled_rhs = jnp.concatenate(
            [r.hub_rows[...].reshape(s.link_cols, width), jnp.ones((s.link_cols, width), BF16)],
            axis=1,
        )
        both = lax.dot_general(r.links[:, cols], pulled_rhs, TALL, preferred_element_type=F32)
        r.near[cols, :] = r.near[cols, :] + both[:, :width]
        r.degree[cols, :] = FAN + both[:, width:]

    loop(chunks, pull_step)

    inputs[6].wait()
    picks = lax.broadcasted_iota(jnp.int32, (2 * chunks, width), 0)

    def forward(i):
        rows = slice(i * CHUNK, (i + 1) * CHUNK)
        pre = r.proj_self[rows, :] + r.near[rows, :] / r.degree[rows, :]
        act = pre * jax.nn.sigmoid(pre)
        r.pre_act[rows, :] = pre
        sums = jnp.zeros((2 * chunks, CHUNK), F32)
        for at, value in ((i, act * act), (chunks + i, act * r.cot[rows, :].astype(F32))):
            sums = sums + lax.dot_general(
                jnp.where(picks == at, 1.0, 0.0),
                value,
                WIDE,
                preferred_element_type=F32,
                precision=lax.Precision.HIGHEST,
            )
        return sums

    def col_sum(buf, row):
        return lambda k: copy(buf.at[y], buf.at[y], r.sems_y, row, k - 1, y_peer(k))

    def by_row(buf):
        sums = buf[0]
        for i in range(1, ys):
            sums = sums + buf[i]
        inv_scale = 1.0 / jnp.sqrt(sums[0:chunks] / s.depth + EPSILON)
        inner = sums[chunks:] * inv_scale / s.depth
        return jnp.transpose(jnp.concatenate([inv_scale, inner], axis=0))

    def backward(i, scales):
        rows = slice(i * CHUNK, (i + 1) * CHUNK)
        pre = r.pre_act[rows, :]
        sig = jax.nn.sigmoid(pre)
        inv = scales[:, i : i + 1]
        inner = scales[:, chunks + i : chunks + i + 1]
        normed = pre * sig * inv
        out[rows, :] = normed.astype(BF16)
        slope = sig * (1.0 + pre * (1.0 - sig))
        grad = (r.cot[rows, :].astype(F32) - normed * inner) * inv * slope
        r.low[rows, :] = grad.astype(BF16)
        r.scaled[rows, :] = (grad / r.degree[rows, :]).astype(BF16)

    sums = forward(1)
    for i in range(2, chunks):
        sums = sums + forward(i)
    r.sums_a[y] = sums
    sum_a = col_sum(r.sums_a, 0)
    each(ys, lambda k: sum_a(k).start())

    each(groups, lambda k: push_g(g_peer(k)[0], k).wait())
    summed = r.push[g, :, width:]
    for k in range(groups - 1):
        summed = summed + r.push_g_in[k].astype(F32)
    r.zsend_g[...] = summed.reshape(zs, HUB_DEV, width)

    def push_gz(k):
        pz, target = z_peer(k)
        return copy(r.zsend_g.at[pz], r.zsend_g_in.at[k - 1], r.sems_z, 2, k - 1, target)

    each(zs, lambda k: push_gz(k).start())

    each(zs, lambda k: push_pz(k).wait())
    hub_sum = r.zsend_p[z]
    for k in range(zs - 1):
        hub_sum = hub_sum + r.zsend_p_in[k]
    count_block = hub_sum[HUB_DEV:]
    lane = lax.broadcasted_iota(jnp.int32, count_block.shape, 1)
    sub = lax.broadcasted_iota(jnp.int32, count_block.shape, 0)
    count_in = jnp.sum(
        jnp.where(lane == sub + z * HUB_DEV, count_block, 0.0), axis=1, keepdims=True
    )
    r.near[0:HUB_DEV, :] = r.near[0:HUB_DEV, :] + hub_sum[0:HUB_DEV]
    r.degree[0:HUB_DEV, :] = r.degree[0:HUB_DEV, :] + count_in
    r.sums_b[y] = forward(0)
    sum_b = col_sum(r.sums_b, 1)
    each(ys, lambda k: sum_b(k).start())

    own_f32 = r.feat[0:16, :].astype(F32)[0:HUB_DEV]
    half = s.depth // 2
    r.hub_feat[z] = jnp.concatenate([own_f32[:, :half], own_f32[:, half:]], axis=0).astype(BF16)

    def gather_f(k):
        mine = r.hub_feat.at[z]
        return copy(mine, mine, r.sems_z, 3, k - 1, z_peer(k)[1])

    each(zs, lambda k: gather_f(k).start())

    def products(lo, hi, first):
        span = slice(lo, hi)

        def add(ref, index, value):
            ref[index] = value if first else ref[index] + value

        def push_step(i):
            rows = pl.ds(pl.multiple_of(i * GROUP_ROWS, GROUP_ROWS), GROUP_ROWS)
            value = jnp.dot(r.links[rows, span], r.scaled[span, :], preferred_element_type=F32)
            add(r.push2, i, value)

        def back_step(i):
            rows = pl.ds(pl.multiple_of(i * CHUNK, CHUNK), CHUNK)
            value = jnp.dot(r.locals_[rows, span], r.scaled[span, :], preferred_element_type=F32)
            add(r.back, (rows, slice(None)), value)

        def self_step(q):
            cols = pl.ds(pl.multiple_of(q * q_rows, q_rows), q_rows)
            value = lax.dot_general(
                r.feat[span, cols], r.low[span, :], TALL, preferred_element_type=F32
            )
            add(r.part, (0, q), value)

        return push_step, back_step, self_step

    each(ys, lambda k: sum_a(k).wait())
    scales = by_row(r.sums_a)
    for i in range(1, chunks):
        backward(i, scales)
    push_step, back_step, self_step = products(CHUNK, nodes, True)
    loop(groups, push_step)
    loop(chunks, back_step)
    loop(xs, self_step)

    each(zs, lambda k: push_gz(k).wait())
    linked = r.zsend_g[z]
    for k in range(zs - 1):
        linked = linked + r.zsend_g_in[k]
    r.own_sum[y] = linked
    spread = col_sum(r.own_sum, 2)
    each(ys, lambda k: spread(k).start())

    each(ys, lambda k: sum_b(k).wait())
    backward(0, by_row(r.sums_b))
    push_step, back_step, self_step = products(0, CHUNK, False)

    def push2(pg, k):
        return copy(r.push2_low.at[pg], r.push2_in.at[k - 1], r.sems_g, 3, k - 1, g_peer(k)[1])

    def push2_to(k):
        pg = g_peer(k)[0]
        push_step(pg)
        r.push2_low[pg] = r.push2[pg, 0:hubs_z].astype(BF16)
        push2(pg, k).start()

    each(groups, push2_to)
    push_step(g)

    def swap(q):
        return copy(r.part.at[1 - c, q], r.part_in.at[q], r.sems_x, 2, q, partner)

    def quarters(body):
        each(xs, lambda k: body(x_peer(k)[0]))
        body(x)

    def self_quarter(q):
        self_step(q)

        @pl.when(c == 1)
        def _():
            swap(q).start()

    quarters(self_quarter)
    loop(chunks, back_step)
    r.back_low[...] = r.back[...].astype(BF16)

    def neigh_quarter(q):
        cols = pl.ds(pl.multiple_of(q * q_rows, q_rows), q_rows)
        r.part[1, q] = lax.dot_general(
            r.feat[:, cols], r.back_low[...], TALL, preferred_element_type=F32
        )

    quarters(neigh_quarter)

    def send_x(k):
        px, target = x_peer(k)
        return copy(r.xsend.at[px], r.xsend_in.at[k - 1], r.sems_x, 0, k - 1, target)

    def open_x():
        def step(k):
            px = x_peer(k)[0]
            swap(px).wait_recv()
            r.xsend[px] = (r.part[c, px] + r.part_in[px]).astype(BF16)
            send_x(k).start()

        each(xs, step)
        swap(x).wait_recv()
        r.total[...] = r.part[c, x] + r.part_in[x]

    @pl.when(c == 0)
    def _():
        open_x()

    each(zs, lambda k: gather_f(k).wait())
    hub_feat = r.hub_feat[...].astype(F32)
    for i in range(2):
        block = hub_feat[:, i * HUB_DEV : (i + 1) * HUB_DEV].reshape(hubs_z, half).astype(BF16)
        r.tall[0:hubs_z, i * half : (i + 1) * half] = block
        r.tall[hubs_z : 2 * hubs_z, i * half : (i + 1) * half] = block
    each(ys, lambda k: spread(k).wait())
    linked = jnp.concatenate([r.own_sum[i] for i in range(ys)], axis=1)
    linked_high = linked.astype(BF16).astype(F32)
    r.tall[2 * hubs_z :, :] = jnp.concatenate([linked_high, linked - linked_high], axis=0).astype(BF16)
    own_scaled = r.scaled[0:16, :].astype(F32)[0:HUB_DEV]
    each(groups, lambda k: push2(g_peer(k)[0], k).wait())
    summed = r.push2[g, 0:hubs_z]
    for k in range(groups - 1):
        summed = summed + r.push2_in[k].astype(F32)
    high = summed.astype(BF16).astype(F32)
    flat = jnp.concatenate([high, summed - high, own_scaled, own_scaled], axis=0).astype(BF16)

    def hub_quarter(q):
        cols = pl.ds(pl.multiple_of(q * q_rows, q_rows), q_rows)
        r.part[1, q] = r.part[1, q] + lax.dot_general(
            r.tall[:, cols], flat, TALL, preferred_element_type=F32
        )

        @pl.when(c == 0)
        def _():
            swap(q).start()

    quarters(hub_quarter)

    @pl.when(c == 1)
    def _():
        open_x()

    each(xs, lambda k: send_x(k).wait())
    reduced = r.total[...]
    for k in range(xs - 1):
        reduced = reduced + r.xsend_in[k].astype(F32)
    r.quarter[...] = reduced.reshape(owners, s.o_rows, width)
    r.zq[...] = reduced.astype(BF16).reshape(owners, s.o_rows, width)

    def owns(pz):
        return lax.rem(pz, 3) != 2

    def rank(pz):
        return (pz // 3) * 2 + lax.rem(pz, 3)

    def send_q(k):
        pz, target = z_peer(k)
        return copy(r.zq.at[rank(pz)], r.zq_in.at[k - 1], r.sems_z, 4, k - 1, target)

    def wait_q(k):
        return copy(r.zq.at[0], r.zq_in.at[k - 1], r.sems_z, 4, k - 1, z_peer(k)[1])

    def send_f(k):
        mine = r.final.at[c, x, rank(z)]
        return copy(mine, mine, r.sems_z, 5, k - 1, z_peer(k)[1])

    def wait_f(k):
        piece = r.final.at[c, x, 0]
        return copy(piece, piece, r.sems_z, 5, k - 1, z_peer(k)[1])

    def send_xf(piece, k):
        mine = r.final.at[c, x, piece]
        return copy(mine, mine, r.sems_f, k - 1, piece, x_peer(k)[1])

    def start_q(k):
        @pl.when(owns(z_peer(k)[0]))
        def _():
            send_q(k).start()

    each(zs, start_q)

    @pl.when(owns(z))
    def _():
        mine = r.quarter[rank(z)]
        each_near(zs, lambda k: wait_q(k).wait_recv())
        for k in range(zs - 1):
            mine = mine + r.zq_in[k].astype(F32)
        r.final[c, x, rank(z)] = mine.astype(BF16)
        each(zs, lambda k: send_f(k).start())
        each(xs, lambda k: send_xf(rank(z), k).start())

    def arrive(k):
        source = lax.rem(z + zs - k, zs)

        @pl.when(owns(source))
        def _():
            wait_f(k).wait_recv()
            each(xs, lambda j: send_xf(rank(source), j).start())

    each_near(zs, arrive)

    def hand_over(k, px):
        piece = r.final.at[c, px]
        return copy(piece, piece, r.sems_x, 1, k, partner)

    hand_over(0, x).start()

    def pass_on(k):
        loop(owners, lambda piece: send_xf(piece, k).wait_recv())
        hand_over(k, lax.rem(x + xs - k, xs)).start()

    each_near(xs, pass_on)

    def finish_q(k):
        @pl.when(owns(z_peer(k)[0]))
        def _():
            wait_q(k).wait_send()

    each(zs, finish_q)

    @pl.when(owns(z))
    def _():
        each(zs, lambda k: wait_f(k).wait_send())

    each(xs, lambda k: loop(owners, lambda piece: send_xf(piece, k).wait_send()))
    loop(xs, lambda q: swap(q).wait_send())
    loop(xs, lambda k: hand_over(k, 0).wait())
    grads[...] = r.final[...].reshape(CORES, s.depth, width)


def local(dims, features, w_self, w_neigh, local_nbr, hub_link, hub_used, cotangent):
    nodes, depth = features.shape
    s = sizes(dims, nodes, depth, w_self.shape[1])
    scratch = scratch_of(s)
    output, grads = pl.pallas_call(
        functools.partial(kernel, s, tuple(scratch)),
        out_shape=(
            jax.ShapeDtypeStruct((nodes, s.width), BF16),
            jax.ShapeDtypeStruct((CORES, depth, s.width), BF16),
        ),
        in_specs=[pl.BlockSpec(memory_space=pl.ANY)] * 7,
        out_specs=(pl.BlockSpec(memory_space=pltpu.VMEM),) * 2,
        scratch_shapes=list(scratch.values()),
        compiler_params=pltpu.CompilerParams(
            collective_id=0, has_side_effects=True, vmem_limit_bytes=56 * 1024 * 1024
        ),
    )(features, w_self, w_neigh, local_nbr.T, hub_link.T, hub_used.T, cotangent)
    return output, grads[0].astype(F32), grads[1].astype(F32)


def solution(mesh):
    ys = mesh.shape["cols"]
    xs = X_CHIPS
    zs = mesh.shape["nodes"] // (xs * CORES)
    placed = (
        P("nodes", None),
        P(None, "cols"),
        P(None, "cols"),
        P("nodes", None),
        P("nodes", None),
        P("nodes", None),
        P("nodes", "cols"),
    )
    return jax.shard_map(
        functools.partial(local, (xs, zs, ys)),
        mesh=mesh,
        in_specs=placed,
        out_specs=(P("nodes", "cols"), P(None, "cols"), P(None, "cols")),
        check_vma=False,
    )
```

time: 1120 us -> 80.1 us (0.07)
  waiting for transfers between devices: 529 us -> 0 us
  blocking collectives: 386 us -> 0 us
  other arithmetic: 127 us -> 2.07 us
  Pallas kernels: 0 us -> 75.5 us
  local copies, waits for them, and re-layouts: 44.3 us -> 1.67 us
  between operations: 14.6 us -> 0.64 us
  matrix products: 13.4 us -> 0 us
    psum x1 -> x0, waiting for transfers between devices: 273 us -> none  [local(): grad_self, grad_neigh = lax.psum((self_part, neigh_part), 'nodes')]
    unnamed x5 -> x0, waiting for transfers between devices: 256 us -> none
    unnamed x1 -> x0, blocking collectives: 196 us -> none
    all_gather x2 -> x0, blocking collectives: 165 us -> none  [hub_parts(): piece = lax.all_gather(own_hubs, 'nodes', axis=0, tiled=True)]
    scatter-add x4 -> x0, other arithmetic: 124 us -> none  [the longest x2 51 us: hub_parts(): jax.ops.segment_sum(spread, hub_link.reshape(-1), num_segments=total_hubs)]
    pallas_call x0 -> x1, Pallas kernels: none -> 75.5 us  [local(): pl.pallas_call(functools.partial(kernel, s, tuple(scratch)), out_shape=(j...]
    gather x8 -> x0, local copies, waits for them, and re-layouts: 32.1 us -> none  [local(): jnp.take(proj_neigh, local_nbr[:, k], axis=0).astype(jnp.float32)]
    psum x2 -> x0, blocking collectives: 25.1 us -> none  [column_total(): return lax.psum(values, 'cols')]
  transfers between devices with their start and end apart: 3 -> 0, of which waited for: 2 -> 0; matrix products, arithmetic and copies ran while one was open for 6% -> 0% of each run, Pallas kernels for 0% -> 0%
where the time goes in v2:
time: 80.1 us; the launch traced here: 79.9 us
  Pallas kernels  75.5 us (94%)
  other arithmetic  2.07 us (3%)
  local copies, waits for them, and re-layouts  1.67 us (2%)
    pallas_call x1, Pallas kernels, local(): pl.pallas_call(functools.partial(kernel, s, tuple(scratch)), out_shape=(j...  75.5 us
    convert_element_type x1, other arithmetic, local(): return (output, grads[0].astype(F32), grads[1].astype(F32))  2.07 us
    unnamed x1, local copies, waits for them, and re-layouts  1.67 us

profile of v2, /device:TPU:1, one launch (start us, length us, event | category | flops | bytes accessed | tf_op | source)
XLA Modules:
  0.0 79.9 jit_solution(1691798550334994075)
XLA Ops:
  0.6 75.5 %shard_map.94 = (bf16[1024,128]{1,0:T(8,128)(2,1)}, bf16[2,1024,128]{2,1,0:T(8,128)(2,1)}) custom-call(bf16[1024,1024]{1,0:T(8,128)(2,1)} %feat_in.1, bf16[1024,128]{1,0:T(8,128)(2,1)} %w_self_in.1, bf16[1024,128]{1,0:T(8,128)(2,1)} %w_neigh_in.1, s32[8,1024]{1,0:T(8,128)} %bitcast.9, s32[4,1024]{1,0:T(4,128)} %bitcast.10, s32[4,1024]{1,0:T(4,128)} %bitcast.11, ...), custom_call_target="tpu_custom_call" | custom-call | tf_op jit(solution)/shard_map/pallas_call | solution.py:639
  76.2 2.1 %bitcast_convert_fusion = (f32[1024,128]{1,0:T(8,128)}, f32[1024,128]{1,0:T(8,128)}) fusion(bf16[2,1024,128]{2,1,0:T(8,128)(2,1)} %get-tuple-element.6), kind=kLoop, calls=%fused_computation | loop fusion | flops 262144 | bytes 1572864 | tf_op jit(solution)/shard_map/convert_element_type | solution.py:652
  78.2 1.7 %copy.11 = bf16[1024,128]{1,0:T(8,128)(2,1)} copy(bf16[1024,128]{1,0:T(8,128)(2,1)} %get-tuple-element.12) | data formatting | bytes 524288

commit v3 on v2

--- a/solution.py
+++ b/solution.py
@@ -40,7 +40,6 @@
     vmem = pltpu.VMEM
     dma = pltpu.SemaphoreType.DMA
     w = s.width
-    sum_rows = 2 * s.chunks
     hub_k = 2 * s.hubs_z + 2 * HUB_DEV
     return {
         "feat": vmem((s.nodes, s.depth), BF16),
@@ -57,26 +56,27 @@
         "hub_rows": vmem((s.groups, GROUP_ROWS, w), BF16),
         "near": vmem((s.nodes, w), F32),
         "degree": vmem((s.nodes, w), F32),
-        "pre_act": vmem((s.nodes, w), F32),
         "push": vmem((s.groups, s.hubs_z, 2 * w), F32),
-        "push_p": vmem((s.groups, s.hubs_z + 16, w), BF16),
-        "push_p_in": vmem((s.groups - 1, s.hubs_z + 16, w), BF16),
+        "push_p": vmem((s.groups, s.hubs_z, w), BF16),
+        "push_p_in": vmem((s.groups - 1, s.hubs_z, w), BF16),
+        "push_c": vmem((s.groups, 2 * HUB_DEV, GROUP_ROWS), BF16),
+        "push_c_in": vmem((s.groups - 1, 2 * HUB_DEV, GROUP_ROWS), BF16),
         "push_g": vmem((s.groups, s.hubs_z, w), BF16),
         "push_g_in": vmem((s.groups - 1, s.hubs_z, w), BF16),
-        "zsend_p": vmem((s.zs, 2 * HUB_DEV, w), F32),
-        "zsend_p_in": vmem((s.zs - 1, 2 * HUB_DEV, w), F32),
+        "zsum_p": vmem((s.zs, HUB_DEV, w), F32),
+        "zsend_p": vmem((s.zs, 2 * HUB_DEV, w), BF16),
+        "zsend_p_in": vmem((s.zs - 1, 2 * HUB_DEV, w), BF16),
         "zsend_g": vmem((s.zs, HUB_DEV, w), F32),
         "zsend_g_in": vmem((s.zs - 1, HUB_DEV, w), F32),
         "own_p": vmem((s.zs, HUB_DEV, w), F32),
         "own_sum": vmem((s.ys, HUB_DEV, w), F32),
         "hub_feat": vmem((s.zs, 2 * HUB_DEV, s.depth // 2), BF16),
-        "sums_a": vmem((s.ys, sum_rows, CHUNK), F32),
-        "sums_b": vmem((s.ys, sum_rows, CHUNK), F32),
-        "low": vmem((s.nodes, w), BF16),
+        "sums": vmem((s.ys, 2 * s.chunks, CHUNK), F32),
+        "act": vmem((s.nodes, w), F32),
+        "act_slope": vmem((s.nodes, w), F32),
+        "cot_slope": vmem((s.nodes, w), F32),
+        "lows": vmem((s.nodes, 2 * w), BF16),
         "scaled": vmem((s.nodes, w), BF16),
-        "back": vmem((s.nodes, w), F32),
-        "back_low": vmem((s.nodes, w), BF16),
-        "push2": vmem((s.groups, GROUP_ROWS, w), F32),
         "push2_low": vmem((s.groups, s.hubs_z, w), BF16),
         "push2_in": vmem((s.groups - 1, s.hubs_z, w), BF16),
         "tall": vmem((hub_k, s.depth), BF16),
@@ -90,8 +90,8 @@
         "zq_in": vmem((s.zs - 1, s.o_rows, w), BF16),
         "final": vmem((CORES, s.xs, s.owners, s.o_rows, w), BF16),
         "sems_z": dma((2, 6, s.zs - 1)),
-        "sems_g": dma((2, 4, s.groups - 1)),
-        "sems_y": dma((2, 3, s.ys - 1)),
+        "sems_g": dma((2, 5, s.groups - 1)),
+        "sems_y": dma((2, 2, s.ys - 1)),
         "sems_x": dma((2, 3, s.xs)),
         "sems_f": dma((2, s.xs - 1, s.owners)),
         "sems_l": dma((7,)),
@@ -162,9 +162,6 @@
     def greet(target):
         pl.semaphore_signal(barrier, inc=1, device_id=target, device_id_type=pl.DeviceIdType.MESH)
 
-    each(zs, lambda k: greet(z_peer(k)[1]))
-    each(ys, lambda k: greet(y_peer(k)))
-    each(groups, lambda k: greet(g_peer(k)[1]))
     inputs = [
         pltpu.make_async_copy(src, dst, r.sems_l.at[i])
         for i, (src, dst) in enumerate(
@@ -181,15 +178,19 @@
     ]
     for item in inputs:
         item.start()
+    each(zs, lambda k: greet(z_peer(k)[1]))
+    each(ys, lambda k: greet(y_peer(k)))
+    each(groups, lambda k: greet(g_peer(k)[1]))
     r.hub_rows[:, hubs_z:] = jnp.zeros((groups, GROUP_ROWS - hubs_z, width), BF16)
 
     def build(dest, base, count, picks):
-        for first in range(0, count, TILE):
-            ids = lax.broadcasted_iota(jnp.int32, (TILE, nodes), 0) + (base + first)
-            acc = jnp.zeros((TILE, nodes), F32)
-            for k in range(picks.shape[0]):
-                acc = acc + jnp.where(ids == picks[k : k + 1, :], 1.0, 0.0)
-            dest[pl.ds(pl.multiple_of(base + first, TILE), TILE), :] = acc.astype(BF16)
+        near_ids = (picks - base).astype(jnp.int16)
+        ids = lax.broadcasted_iota(jnp.int16, (count, nodes), 0)
+        acc = jnp.zeros((count, nodes), BF16)
+        for k in range(picks.shape[0]):
+            hit = ids == near_ids[k : k + 1, :]
+            acc = acc + jnp.where(hit, jnp.bfloat16(1.0), jnp.bfloat16(0.0))
+        dest[pl.ds(pl.multiple_of(base, GROUP_ROWS), count), :] = acc
 
     inputs[0].wait()
     inputs[1].wait()
@@ -219,13 +220,10 @@
     inputs[3].wait()
     own_rows = r.feat[0:16, :]
     r.own_p[z] = jnp.dot(own_rows, r.w_neigh[...], preferred_element_type=F32)[0:HUB_DEV]
-    pl.semaphore_wait(barrier, zs + groups + ys - 3)
 
     def gather_z(k):
         mine = r.own_p.at[z]
         return copy(mine, mine, r.sems_z, 0, k - 1, z_peer(k)[1])
-
-    each(zs, lambda k: gather_z(k).start())
 
     def proj_step(i):
         rows = pl.ds(pl.multiple_of(i * CHUNK, CHUNK), CHUNK)
@@ -235,7 +233,6 @@
         r.pushable[rows, width:] = r.feat[rows, pl.ds(pl.multiple_of(y * width, 128), width)]
 
     loop(chunks, proj_step)
-    node_ones = jnp.ones((HUB_DEV, nodes), BF16)
 
     def push_p(pg, k):
         target = g_peer(k)[1]
@@ -245,48 +242,52 @@
         target = g_peer(k)[1]
         return copy(r.push_g.at[pg], r.push_g_in.at[k - 1], r.sems_g, 1, k - 1, target)
 
+    def push_c(pg, k):
+        target = g_peer(k)[1]
+        return copy(r.push_c.at[pg], r.push_c_in.at[k - 1], r.sems_g, 4, k - 1, target)
+
     def push_rows(pg):
         rows = r.links[pl.ds(pl.multiple_of(pg * GROUP_ROWS, GROUP_ROWS), GROUP_ROWS), :]
         both = jnp.dot(rows, r.pushable[...], preferred_element_type=F32)[0:hubs_z]
-        count = lax.dot_general(node_ones, rows, WIDE, preferred_element_type=F32)
-        count_high = count.astype(BF16).astype(F32)
-        counts = jnp.concatenate([count_high, count - count_high], axis=0)
         r.push[pg] = both
-        r.push_p[pg, 0:hubs_z] = both[:, :width].astype(BF16)
-        r.push_p[pg, hubs_z:] = counts.astype(BF16)
+        r.push_p[pg] = both[:, :width].astype(BF16)
         r.push_g[pg] = both[:, width:].astype(BF16)
 
-    def push_to(k):
-        pg = g_peer(k)[0]
-        push_rows(pg)
-        push_p(pg, k).start()
-
-    each(groups, push_to)
-    push_rows(g)
+    loop(groups, push_rows)
+    pl.semaphore_wait(barrier, zs + groups + ys - 3)
+    each(zs, lambda k: gather_z(k).start())
+    each(groups, lambda k: push_p(g_peer(k)[0], k).start())
+
+    def split_count(count):
+        high = count.astype(BF16).astype(F32)
+        return jnp.concatenate([high, count - high], axis=0).astype(BF16)
+
+    count = lax.dot_general(
+        jnp.ones((HUB_DEV, nodes), BF16), r.links[...], WIDE, preferred_element_type=F32
+    )
+    for i in range(groups):
+        r.push_c[i] = split_count(count[:, i * GROUP_ROWS : (i + 1) * GROUP_ROWS])
+    each(groups, lambda k: push_c(g_peer(k)[0], k).start())
     each(groups, lambda k: push_g(g_peer(k)[0], k).start())
 
-    each(zs, lambda k: gather_z(k).wait())
-    r.hub_rows[g, 0:hubs_z] = r.own_p[...].reshape(hubs_z, width).astype(BF16)
-
-    def gather_g(k):
-        mine = r.hub_rows.at[g, pl.ds(0, hubs_z)]
-        return copy(mine, mine, r.sems_g, 2, k - 1, g_peer(k)[1])
-
-    each(groups, lambda k: gather_g(k).start())
-
     inputs[5].wait()
-    loop(nodes // 128, lambda i: build(r.locals_, i * 128, 128, r.nbr[...]))
+    loop(nodes // GROUP_ROWS, lambda i: build(r.locals_, i * GROUP_ROWS, GROUP_ROWS, r.nbr[...]))
 
     each(groups, lambda k: push_p(g_peer(k)[0], k).wait())
+    each(groups, lambda k: push_c(g_peer(k)[0], k).wait())
     summed = r.push[g, :, 0:width]
-    counts = r.push_p[g, hubs_z:].astype(F32)
+    counts = r.push_c[g].astype(F32)
     for k in range(groups - 1):
-        summed = summed + r.push_p_in[k, 0:hubs_z].astype(F32)
-        counts = counts + r.push_p_in[k, hubs_z:].astype(F32)
+        summed = summed + r.push_p_in[k].astype(F32)
+        counts = counts + r.push_c_in[k].astype(F32)
     counts = counts[0:HUB_DEV] + counts[HUB_DEV:]
+    high = counts.astype(BF16).astype(F32)
+    part_row = lax.broadcasted_iota(jnp.int32, counts.shape, 0)
+    parts = jnp.where(part_row == 0, high, jnp.where(part_row == 1, counts - high, 0.0))
+    r.zsum_p[...] = summed.reshape(zs, HUB_DEV, width)
     for i in range(zs):
-        r.zsend_p[i, 0:HUB_DEV] = summed[i * HUB_DEV : (i + 1) * HUB_DEV]
-        r.zsend_p[i, HUB_DEV:] = counts
+        rows = summed[i * HUB_DEV : (i + 1) * HUB_DEV]
+        r.zsend_p[i] = jnp.concatenate([rows, parts], axis=0).astype(BF16)
 
     def push_pz(k):
         pz, target = z_peer(k)
@@ -302,33 +303,60 @@
         r.near[rows, :] = lax.dot_general(
             r.locals_[:, rows], r.pushable[:, 0:width], TALL, preferred_element_type=F32
         )
+        r.degree[rows, :] = FAN + lax.dot_general(
+            r.links[:, rows], jnp.ones((s.link_cols, width), BF16), TALL, preferred_element_type=F32
+        )
 
     loop(chunks, near_step)
 
+    each(zs, lambda k: gather_z(k).wait())
+    r.hub_rows[g, 0:hubs_z] = r.own_p[...].reshape(hubs_z, width).astype(BF16)
+
+    def gather_g(k):
+        mine = r.hub_rows.at[g, pl.ds(0, hubs_z)]
+        return copy(mine, mine, r.sems_g, 2, k - 1, g_peer(k)[1])
+
+    each(groups, lambda k: gather_g(k).start())
+
+    each(groups, lambda k: push_g(g_peer(k)[0], k).wait())
+    summed = r.push[g, :, width:]
+    for k in range(groups - 1):
+        summed = summed + r.push_g_in[k].astype(F32)
+    r.zsend_g[...] = summed.reshape(zs, HUB_DEV, width)
+
+    def push_gz(k):
+        pz, target = z_peer(k)
+        return copy(r.zsend_g.at[pz], r.zsend_g_in.at[k - 1], r.sems_z, 2, k - 1, target)
+
+    each(zs, lambda k: push_gz(k).start())
+
     each(groups, lambda k: gather_g(k).wait())
-
-    def pull_step(i):
-        cols = pl.ds(pl.multiple_of(i * CHUNK, CHUNK), CHUNK)
-        pulled_rhs = jnp.concatenate(
-            [r.hub_rows[...].reshape(s.link_cols, width), jnp.ones((s.link_cols, width), BF16)],
-            axis=1,
+    inputs[6].wait()
+
+    def pull(i):
+        rows = slice(i * CHUNK, (i + 1) * CHUNK)
+        r.near[rows, :] = r.near[rows, :] + lax.dot_general(
+            r.links[:, rows],
+            r.hub_rows[...].reshape(s.link_cols, width),
+            TALL,
+            preferred_element_type=F32,
         )
-        both = lax.dot_general(r.links[:, cols], pulled_rhs, TALL, preferred_element_type=F32)
-        r.near[cols, :] = r.near[cols, :] + both[:, :width]
-        r.degree[cols, :] = FAN + both[:, width:]
-
-    loop(chunks, pull_step)
-
-    inputs[6].wait()
-    picks = lax.broadcasted_iota(jnp.int32, (2 * chunks, width), 0)
-
-    def forward(i):
+
+    def activate(i):
         rows = slice(i * CHUNK, (i + 1) * CHUNK)
-        pre = r.proj_self[rows, :] + r.near[rows, :] / r.degree[rows, :]
-        act = pre * jax.nn.sigmoid(pre)
-        r.pre_act[rows, :] = pre
+        picks = lax.broadcasted_iota(jnp.int32, (2 * chunks, width), 0)
+        per_degree = 1.0 / r.degree[rows, :]
+        pre = r.proj_self[rows, :] + r.near[rows, :] * per_degree
+        sig = jax.nn.sigmoid(pre)
+        act = pre * sig
+        slope = sig * (1.0 + pre * (1.0 - sig))
+        cot = r.cot[rows, :].astype(F32)
+        r.degree[rows, :] = per_degree
+        r.act[rows, :] = act
+        r.act_slope[rows, :] = act * slope
+        r.cot_slope[rows, :] = cot * slope
         sums = jnp.zeros((2 * chunks, CHUNK), F32)
-        for at, value in ((i, act * act), (chunks + i, act * r.cot[rows, :].astype(F32))):
+        for at, value in ((i, act * act), (chunks + i, act * cot)):
             sums = sums + lax.dot_general(
                 jnp.where(picks == at, 1.0, 0.0),
                 value,
@@ -338,64 +366,32 @@
             )
         return sums
 
+    sums = jnp.zeros((2 * chunks, CHUNK), F32)
+    for i in range(1, chunks):
+        pull(i)
+        sums = sums + activate(i)
+    pull(0)
+
+    each(zs, lambda k: push_pz(k).wait())
+    inflow = r.zsum_p[z]
+    counts = r.zsend_p[z].astype(F32)[HUB_DEV:]
+    for k in range(zs - 1):
+        block = r.zsend_p_in[k].astype(F32)
+        inflow = inflow + block[0:HUB_DEV]
+        counts = counts + block[HUB_DEV:]
+    counts = jnp.sum(counts, axis=0, keepdims=True)
+    lane = lax.broadcasted_iota(jnp.int32, (HUB_DEV, GROUP_ROWS), 1)
+    sub = lax.broadcasted_iota(jnp.int32, (HUB_DEV, GROUP_ROWS), 0)
+    count_in = jnp.sum(jnp.where(lane == sub + z * HUB_DEV, counts, 0.0), axis=1, keepdims=True)
+    r.near[0:HUB_DEV, :] = r.near[0:HUB_DEV, :] + inflow
+    r.degree[0:HUB_DEV, :] = r.degree[0:HUB_DEV, :] + count_in
+    r.sums[y] = sums + activate(0)
+
     def col_sum(buf, row):
         return lambda k: copy(buf.at[y], buf.at[y], r.sems_y, row, k - 1, y_peer(k))
 
-    def by_row(buf):
-        sums = buf[0]
-        for i in range(1, ys):
-            sums = sums + buf[i]
-        inv_scale = 1.0 / jnp.sqrt(sums[0:chunks] / s.depth + EPSILON)
-        inner = sums[chunks:] * inv_scale / s.depth
-        return jnp.transpose(jnp.concatenate([inv_scale, inner], axis=0))
-
-    def backward(i, scales):
-        rows = slice(i * CHUNK, (i + 1) * CHUNK)
-        pre = r.pre_act[rows, :]
-        sig = jax.nn.sigmoid(pre)
-        inv = scales[:, i : i + 1]
-        inner = scales[:, chunks + i : chunks + i + 1]
-        normed = pre * sig * inv
-        out[rows, :] = normed.astype(BF16)
-        slope = sig * (1.0 + pre * (1.0 - sig))
-        grad = (r.cot[rows, :].astype(F32) - normed * inner) * inv * slope
-        r.low[rows, :] = grad.astype(BF16)
-        r.scaled[rows, :] = (grad / r.degree[rows, :]).astype(BF16)
-
-    sums = forward(1)
-    for i in range(2, chunks):
-        sums = sums + forward(i)
-    r.sums_a[y] = sums
-    sum_a = col_sum(r.sums_a, 0)
-    each(ys, lambda k: sum_a(k).start())
-
-    each(groups, lambda k: push_g(g_peer(k)[0], k).wait())
-    summed = r.push[g, :, width:]
-    for k in range(groups - 1):
-        summed = summed + r.push_g_in[k].astype(F32)
-    r.zsend_g[...] = summed.reshape(zs, HUB_DEV, width)
-
-    def push_gz(k):
-        pz, target = z_peer(k)
-        return copy(r.zsend_g.at[pz], r.zsend_g_in.at[k - 1], r.sems_z, 2, k - 1, target)
-
-    each(zs, lambda k: push_gz(k).start())
-
-    each(zs, lambda k: push_pz(k).wait())
-    hub_sum = r.zsend_p[z]
-    for k in range(zs - 1):
-        hub_sum = hub_sum + r.zsend_p_in[k]
-    count_block = hub_sum[HUB_DEV:]
-    lane = lax.broadcasted_iota(jnp.int32, count_block.shape, 1)
-    sub = lax.broadcasted_iota(jnp.int32, count_block.shape, 0)
-    count_in = jnp.sum(
-        jnp.where(lane == sub + z * HUB_DEV, count_block, 0.0), axis=1, keepdims=True
-    )
-    r.near[0:HUB_DEV, :] = r.near[0:HUB_DEV, :] + hub_sum[0:HUB_DEV]
-    r.degree[0:HUB_DEV, :] = r.degree[0:HUB_DEV, :] + count_in
-    r.sums_b[y] = forward(0)
-    sum_b = col_sum(r.sums_b, 1)
-    each(ys, lambda k: sum_b(k).start())
+    col_sums = col_sum(r.sums, 0)
+    each(ys, lambda k: col_sums(k).start())
 
     own_f32 = r.feat[0:16, :].astype(F32)[0:HUB_DEV]
     half = s.depth // 2
@@ -406,64 +402,54 @@
         return copy(mine, mine, r.sems_z, 3, k - 1, z_peer(k)[1])
 
     each(zs, lambda k: gather_f(k).start())
-
-    def products(lo, hi, first):
-        span = slice(lo, hi)
-
-        def add(ref, index, value):
-            ref[index] = value if first else ref[index] + value
-
-        def push_step(i):
-            rows = pl.ds(pl.multiple_of(i * GROUP_ROWS, GROUP_ROWS), GROUP_ROWS)
-            value = jnp.dot(r.links[rows, span], r.scaled[span, :], preferred_element_type=F32)
-            add(r.push2, i, value)
-
-        def back_step(i):
-            rows = pl.ds(pl.multiple_of(i * CHUNK, CHUNK), CHUNK)
-            value = jnp.dot(r.locals_[rows, span], r.scaled[span, :], preferred_element_type=F32)
-            add(r.back, (rows, slice(None)), value)
-
-        def self_step(q):
-            cols = pl.ds(pl.multiple_of(q * q_rows, q_rows), q_rows)
-            value = lax.dot_general(
-                r.feat[span, cols], r.low[span, :], TALL, preferred_element_type=F32
-            )
-            add(r.part, (0, q), value)
-
-        return push_step, back_step, self_step
-
-    each(ys, lambda k: sum_a(k).wait())
-    scales = by_row(r.sums_a)
-    for i in range(1, chunks):
-        backward(i, scales)
-    push_step, back_step, self_step = products(CHUNK, nodes, True)
-    loop(groups, push_step)
-    loop(chunks, back_step)
-    loop(xs, self_step)
 
     each(zs, lambda k: push_gz(k).wait())
     linked = r.zsend_g[z]
     for k in range(zs - 1):
         linked = linked + r.zsend_g_in[k]
     r.own_sum[y] = linked
-    spread = col_sum(r.own_sum, 2)
+    spread = col_sum(r.own_sum, 1)
     each(ys, lambda k: spread(k).start())
 
-    each(ys, lambda k: sum_b(k).wait())
-    backward(0, by_row(r.sums_b))
-    push_step, back_step, self_step = products(0, CHUNK, False)
+    each(ys, lambda k: col_sums(k).wait())
+    sums = r.sums[0]
+    for i in range(1, ys):
+        sums = sums + r.sums[i]
+    inv_scale = 1.0 / jnp.sqrt(sums[0:chunks] / s.depth + EPSILON)
+    inner = sums[chunks:] * inv_scale / s.depth
+    scales = jnp.transpose(jnp.concatenate([inv_scale, inv_scale * inv_scale * inner], axis=0))
+    for i in range(chunks):
+        rows = slice(i * CHUNK, (i + 1) * CHUNK)
+        grad = (
+            r.cot_slope[rows, :] * scales[:, i : i + 1]
+            - r.act_slope[rows, :] * scales[:, chunks + i : chunks + i + 1]
+        )
+        r.lows[rows, 0:width] = grad.astype(BF16)
+        r.scaled[rows, :] = (grad * r.degree[rows, :]).astype(BF16)
 
     def push2(pg, k):
         return copy(r.push2_low.at[pg], r.push2_in.at[k - 1], r.sems_g, 3, k - 1, g_peer(k)[1])
 
+    def push2_rows(pg):
+        rows = pl.ds(pl.multiple_of(pg * GROUP_ROWS, GROUP_ROWS), GROUP_ROWS)
+        value = jnp.dot(r.links[rows, :], r.scaled[...], preferred_element_type=F32)
+        return value[0:hubs_z]
+
     def push2_to(k):
         pg = g_peer(k)[0]
-        push_step(pg)
-        r.push2_low[pg] = r.push2[pg, 0:hubs_z].astype(BF16)
+        r.push2_low[pg] = push2_rows(pg).astype(BF16)
         push2(pg, k).start()
 
     each(groups, push2_to)
-    push_step(g)
+    own_push2 = push2_rows(g)
+
+    def back_step(i):
+        rows = pl.ds(pl.multiple_of(i * CHUNK, CHUNK), CHUNK)
+        r.lows[rows, width:] = jnp.dot(
+            r.locals_[rows, :], r.scaled[...], preferred_element_type=F32
+        ).astype(BF16)
+
+    loop(chunks, back_step)
 
     def swap(q):
         return copy(r.part.at[1 - c, q], r.part_in.at[q], r.sems_x, 2, q, partner)
@@ -472,24 +458,17 @@
         each(xs, lambda k: body(x_peer(k)[0]))
         body(x)
 
-    def self_quarter(q):
-        self_step(q)
+    def grad_quarter(q):
+        cols = pl.ds(pl.multiple_of(q * q_rows, q_rows), q_rows)
+        both = lax.dot_general(r.feat[:, cols], r.lows[...], TALL, preferred_element_type=F32)
+        r.part[0, q] = both[:, :width]
+        r.part[1, q] = both[:, width:]
 
         @pl.when(c == 1)
         def _():
             swap(q).start()
 
-    quarters(self_quarter)
-    loop(chunks, back_step)
-    r.back_low[...] = r.back[...].astype(BF16)
-
-    def neigh_quarter(q):
-        cols = pl.ds(pl.multiple_of(q * q_rows, q_rows), q_rows)
-        r.part[1, q] = lax.dot_general(
-            r.feat[:, cols], r.back_low[...], TALL, preferred_element_type=F32
-        )
-
-    quarters(neigh_quarter)
+    quarters(grad_quarter)
 
     def send_x(k):
         px, target = x_peer(k)
@@ -522,7 +501,7 @@
     r.tall[2 * hubs_z :, :] = jnp.concatenate([linked_high, linked - linked_high], axis=0).astype(BF16)
     own_scaled = r.scaled[0:16, :].astype(F32)[0:HUB_DEV]
     each(groups, lambda k: push2(g_peer(k)[0], k).wait())
-    summed = r.push2[g, 0:hubs_z]
+    summed = own_push2
     for k in range(groups - 1):
         summed = summed + r.push2_in[k].astype(F32)
     high = summed.astype(BF16).astype(F32)
@@ -543,6 +522,10 @@
     @pl.when(c == 1)
     def _():
         open_x()
+
+    for i in range(chunks):
+        rows = slice(i * CHUNK, (i + 1) * CHUNK)
+        out[rows, :] = (r.act[rows, :] * scales[:, i : i + 1]).astype(BF16)
 
     each(xs, lambda k: send_x(k).wait())
     reduced = r.total[...]
@@ -630,6 +613,29 @@
     loop(xs, lambda q: swap(q).wait_send())
     loop(xs, lambda k: hand_over(k, 0).wait())
     grads[...] = r.final[...].reshape(CORES, s.depth, width)
+
+
+def finish(output_in, grads_in, output_out, self_out, neigh_out, rows, low, high, sems):
+    count, half = low.shape[0], low.shape[1]
+    loads = []
+    stores = []
+    for i in range(count):
+        part = pl.ds(i % 2 * half, half)
+        target = (self_out, neigh_out)[i // 2]
+        loads.append(pltpu.make_async_copy(grads_in.at[i // 2, part], low.at[i], sems.at[0, i]))
+        stores.append(pltpu.make_async_copy(high.at[i], target.at[part], sems.at[1, i]))
+    loads.append(pltpu.make_async_copy(output_in, rows, sems.at[0, count]))
+    stores.append(pltpu.make_async_copy(rows, output_out, sems.at[1, count]))
+    for load in loads:
+        load.start()
+    for i in range(count):
+        loads[i].wait()
+        high[i] = low[i].astype(F32)
+        stores[i].start()
+    loads[count].wait()
+    stores[count].start()
+    for store in stores:
+        store.wait()
 
 
 def local(dims, features, w_self, w_neigh, local_nbr, hub_link, hub_used, cotangent):
@@ -649,7 +655,19 @@
             collective_id=0, has_side_effects=True, vmem_limit_bytes=56 * 1024 * 1024
         ),
     )(features, w_self, w_neigh, local_nbr.T, hub_link.T, hub_used.T, cotangent)
-    return output, grads[0].astype(F32), grads[1].astype(F32)
+    grad = jax.ShapeDtypeStruct((depth, s.width), F32)
+    return pl.pallas_call(
+        finish,
+        out_shape=(jax.ShapeDtypeStruct((nodes, s.width), BF16), grad, grad),
+        in_specs=[pl.BlockSpec(memory_space=pl.ANY)] * 2,
+        out_specs=(pl.BlockSpec(memory_space=pl.ANY),) * 3,
+        scratch_shapes=[
+            pltpu.VMEM((nodes, s.width), BF16),
+            pltpu.VMEM((2 * CORES, depth // 2, s.width), BF16),
+            pltpu.VMEM((2 * CORES, depth // 2, s.width), F32),
+            pltpu.SemaphoreType.DMA((2, 2 * CORES + 1)),
+        ],
+    )(output, grads)
 
 
 def solution(mesh):

time: 80.1 us -> 75.3 us (0.940)
  other arithmetic: 2.07 us -> 0 us
  local copies, waits for them, and re-layouts: 1.67 us -> 0 us
  Pallas kernels: 75.5 us -> 74.4 us
    pallas_call x1, Pallas kernels: 75.5 us -> 72.4 us  [local(): pl.pallas_call(functools.partial(kernel, s, tuple(scratch)), out_shape=(j...]
    convert_element_type x1 -> x0, other arithmetic: 2.07 us -> none  [local(): return (output, grads[0].astype(F32), grads[1].astype(F32))]
    pallas_call x0 -> x1, Pallas kernels: none -> 2.06 us  [local(): pl.pallas_call(finish, out_shape=(jax.ShapeDtypeStruct((nodes, s.width),...]
    unnamed x1 -> x0, local copies, waits for them, and re-layouts: 1.67 us -> none
where the time goes in v3:
time: 75.3 us; the launch traced here: 75.1 us
  Pallas kernels  74.4 us (99%)
    pallas_call x1, Pallas kernels, local(): pl.pallas_call(functools.partial(kernel, s, tuple(scratch)), out_shape=(j...  72.4 us
    pallas_call x1, Pallas kernels, local(): pl.pallas_call(finish, out_shape=(jax.ShapeDtypeStruct((nodes, s.width),...  2.06 us

profile of v3, /device:TPU:1, one launch (start us, length us, event | category | flops | bytes accessed | tf_op | source)
XLA Modules:
  0.0 75.1 jit_solution(998374480471487158)
XLA Ops:
  0.6 72.4 %shard_map.94 = (bf16[1024,128]{1,0:T(8,128)(2,1)}, bf16[2,1024,128]{2,1,0:T(8,128)(2,1)}) custom-call(bf16[1024,1024]{1,0:T(8,128)(2,1)} %feat_in.1, bf16[1024,128]{1,0:T(8,128)(2,1)} %w_self_in.1, bf16[1024,128]{1,0:T(8,128)(2,1)} %w_neigh_in.1, s32[8,1024]{1,0:T(8,128)} %bitcast.3, s32[4,1024]{1,0:T(4,128)} %bitcast.4, s32[4,1024]{1,0:T(4,128)} %bitcast.5, ...), custom_call_target="tpu_custom_call" | custom-call | tf_op jit(solution)/shard_map/pallas_call | solution.py:645
  73.0 2.1 %shard_map.95 = (bf16[1024,128]{1,0:T(8,128)(2,1)}, f32[1024,128]{1,0:T(8,128)}, f32[1024,128]{1,0:T(8,128)}) custom-call(bf16[1024,128]{1,0:T(8,128)(2,1)} %get-tuple-element.5.output_in, bf16[2,1024,128]{2,1,0:T(8,128)(2,1)} %get-tuple-element.6.grads_in), custom_call_target="tpu_custom_call" | custom-call | tf_op jit(solution)/shard_map/pallas_call | solution.py:659

commit v4 on v3

--- a/solution.py
+++ b/solution.py
@@ -94,7 +94,9 @@
         "sems_y": dma((2, 2, s.ys - 1)),
         "sems_x": dma((2, 3, s.xs)),
         "sems_f": dma((2, s.xs - 1, s.owners)),
-        "sems_l": dma((7,)),
+        "output": vmem((s.nodes, w), BF16),
+        "sems_l": dma((8,)),
+        "sems_o": dma((CORES, s.xs)),
     }
 
 
@@ -273,8 +275,19 @@
     inputs[5].wait()
     loop(nodes // GROUP_ROWS, lambda i: build(r.locals_, i * GROUP_ROWS, GROUP_ROWS, r.nbr[...]))
 
-    each(groups, lambda k: push_p(g_peer(k)[0], k).wait())
-    each(groups, lambda k: push_c(g_peer(k)[0], k).wait())
+    inputs[4].wait()
+
+    def self_step(i):
+        rows = pl.ds(pl.multiple_of(i * CHUNK, CHUNK), CHUNK)
+        r.proj_self[rows, :] = jnp.dot(r.feat[rows, :], r.w_self[...], preferred_element_type=F32)
+        r.degree[rows, :] = FAN + lax.dot_general(
+            r.links[:, rows], jnp.ones((s.link_cols, width), BF16), TALL, preferred_element_type=F32
+        )
+
+    loop(chunks, self_step)
+
+    each(groups, lambda k: push_p(g_peer(k)[0], k).wait_recv())
+    each(groups, lambda k: push_c(g_peer(k)[0], k).wait_recv())
     summed = r.push[g, :, 0:width]
     counts = r.push_c[g].astype(F32)
     for k in range(groups - 1):
@@ -295,30 +308,24 @@
 
     each(zs, lambda k: push_pz(k).start())
 
-    inputs[4].wait()
+    each(zs, lambda k: gather_z(k).wait_recv())
+    r.hub_rows[g, 0:hubs_z] = r.own_p[...].reshape(hubs_z, width).astype(BF16)
+
+    def gather_g(k):
+        mine = r.hub_rows.at[g, pl.ds(0, hubs_z)]
+        return copy(mine, mine, r.sems_g, 2, k - 1, g_peer(k)[1])
+
+    each(groups, lambda k: gather_g(k).start())
 
     def near_step(i):
         rows = pl.ds(pl.multiple_of(i * CHUNK, CHUNK), CHUNK)
-        r.proj_self[rows, :] = jnp.dot(r.feat[rows, :], r.w_self[...], preferred_element_type=F32)
         r.near[rows, :] = lax.dot_general(
             r.locals_[:, rows], r.pushable[:, 0:width], TALL, preferred_element_type=F32
         )
-        r.degree[rows, :] = FAN + lax.dot_general(
-            r.links[:, rows], jnp.ones((s.link_cols, width), BF16), TALL, preferred_element_type=F32
-        )
 
     loop(chunks, near_step)
 
-    each(zs, lambda k: gather_z(k).wait())
-    r.hub_rows[g, 0:hubs_z] = r.own_p[...].reshape(hubs_z, width).astype(BF16)
-
-    def gather_g(k):
-        mine = r.hub_rows.at[g, pl.ds(0, hubs_z)]
-        return copy(mine, mine, r.sems_g, 2, k - 1, g_peer(k)[1])
-
-    each(groups, lambda k: gather_g(k).start())
-
-    each(groups, lambda k: push_g(g_peer(k)[0], k).wait())
+    each(groups, lambda k: push_g(g_peer(k)[0], k).wait_recv())
     summed = r.push[g, :, width:]
     for k in range(groups - 1):
         summed = summed + r.push_g_in[k].astype(F32)
@@ -330,7 +337,7 @@
 
     each(zs, lambda k: push_gz(k).start())
 
-    each(groups, lambda k: gather_g(k).wait())
+    each(groups, lambda k: gather_g(k).wait_recv())
     inputs[6].wait()
 
     def pull(i):
@@ -372,7 +379,7 @@
         sums = sums + activate(i)
     pull(0)
 
-    each(zs, lambda k: push_pz(k).wait())
+    each(zs, lambda k: push_pz(k).wait_recv())
     inflow = r.zsum_p[z]
     counts = r.zsend_p[z].astype(F32)[HUB_DEV:]
     for k in range(zs - 1):
@@ -403,7 +410,7 @@
 
     each(zs, lambda k: gather_f(k).start())
 
-    each(zs, lambda k: push_gz(k).wait())
+    each(zs, lambda k: push_gz(k).wait_recv())
     linked = r.zsend_g[z]
     for k in range(zs - 1):
         linked = linked + r.zsend_g_in[k]
@@ -411,7 +418,7 @@
     spread = col_sum(r.own_sum, 1)
     each(ys, lambda k: spread(k).start())
 
-    each(ys, lambda k: col_sums(k).wait())
+    each(ys, lambda k: col_sums(k).wait_recv())
     sums = r.sums[0]
     for i in range(1, ys):
         sums = sums + r.sums[i]
@@ -489,18 +496,18 @@
     def _():
         open_x()
 
-    each(zs, lambda k: gather_f(k).wait())
+    each(zs, lambda k: gather_f(k).wait_recv())
     hub_feat = r.hub_feat[...].astype(F32)
     for i in range(2):
         block = hub_feat[:, i * HUB_DEV : (i + 1) * HUB_DEV].reshape(hubs_z, half).astype(BF16)
         r.tall[0:hubs_z, i * half : (i + 1) * half] = block
         r.tall[hubs_z : 2 * hubs_z, i * half : (i + 1) * half] = block
-    each(ys, lambda k: spread(k).wait())
+    each(ys, lambda k: spread(k).wait_recv())
     linked = jnp.concatenate([r.own_sum[i] for i in range(ys)], axis=1)
     linked_high = linked.astype(BF16).astype(F32)
     r.tall[2 * hubs_z :, :] = jnp.concatenate([linked_high, linked - linked_high], axis=0).astype(BF16)
     own_scaled = r.scaled[0:16, :].astype(F32)[0:HUB_DEV]
-    each(groups, lambda k: push2(g_peer(k)[0], k).wait())
+    each(groups, lambda k: push2(g_peer(k)[0], k).wait_recv())
     summed = own_push2
     for k in range(groups - 1):
         summed = summed + r.push2_in[k].astype(F32)
@@ -525,9 +532,12 @@
 
     for i in range(chunks):
         rows = slice(i * CHUNK, (i + 1) * CHUNK)
-        out[rows, :] = (r.act[rows, :] * scales[:, i : i + 1]).astype(BF16)
-
-    each(xs, lambda k: send_x(k).wait())
+        r.output[rows, :] = (r.act[rows, :] * scales[:, i : i + 1]).astype(BF16)
+
+    put_output = pltpu.make_async_copy(r.output, out, r.sems_l.at[7])
+    put_output.start()
+
+    each(xs, lambda k: send_x(k).wait_recv())
     reduced = r.total[...]
     for k in range(xs - 1):
         reduced = reduced + r.xsend_in[k].astype(F32)
@@ -565,6 +575,19 @@
             send_q(k).start()
 
     each(zs, start_q)
+
+    each(zs, lambda k: gather_z(k).wait_send())
+    each(groups, lambda k: push_p(g_peer(k)[0], k).wait_send())
+    each(groups, lambda k: push_c(g_peer(k)[0], k).wait_send())
+    each(groups, lambda k: push_g(g_peer(k)[0], k).wait_send())
+    each(groups, lambda k: gather_g(k).wait_send())
+    each(zs, lambda k: push_pz(k).wait_send())
+    each(zs, lambda k: push_gz(k).wait_send())
+    each(ys, lambda k: col_sums(k).wait_send())
+    each(zs, lambda k: gather_f(k).wait_send())
+    each(ys, lambda k: spread(k).wait_send())
+    each(groups, lambda k: push2(g_peer(k)[0], k).wait_send())
+    each(xs, lambda k: send_x(k).wait_send())
 
     @pl.when(owns(z))
     def _():
@@ -590,11 +613,17 @@
         piece = r.final.at[c, px]
         return copy(piece, piece, r.sems_x, 1, k, partner)
 
+    def keep(core, px):
+        return pltpu.make_async_copy(r.final.at[core, px], grads.at[core, px], r.sems_o.at[core, px])
+
     hand_over(0, x).start()
+    keep(c, x).start()
 
     def pass_on(k):
         loop(owners, lambda piece: send_xf(piece, k).wait_recv())
-        hand_over(k, lax.rem(x + xs - k, xs)).start()
+        px = lax.rem(x + xs - k, xs)
+        hand_over(k, px).start()
+        keep(c, px).start()
 
     each_near(xs, pass_on)
 
@@ -611,8 +640,16 @@
 
     each(xs, lambda k: loop(owners, lambda piece: send_xf(piece, k).wait_send()))
     loop(xs, lambda q: swap(q).wait_send())
-    loop(xs, lambda k: hand_over(k, 0).wait())
-    grads[...] = r.final[...].reshape(CORES, s.depth, width)
+    put_output.wait()
+
+    def take(k):
+        hand_over(k, 0).wait()
+        keep(1 - c, lax.rem(x + xs - k, xs)).start()
+
+    take(0)
+    each_near(xs, take)
+    for core in range(CORES):
+        loop(xs, lambda px: keep(core, px).wait())
 
 
 def finish(output_in, grads_in, output_out, self_out, neigh_out, rows, low, high, sems):
@@ -646,10 +683,10 @@
         functools.partial(kernel, s, tuple(scratch)),
         out_shape=(
             jax.ShapeDtypeStruct((nodes, s.width), BF16),
-            jax.ShapeDtypeStruct((CORES, depth, s.width), BF16),
+            jax.ShapeDtypeStruct((CORES, s.xs, s.owners, s.o_rows, s.width), BF16),
         ),
         in_specs=[pl.BlockSpec(memory_space=pl.ANY)] * 7,
-        out_specs=(pl.BlockSpec(memory_space=pltpu.VMEM),) * 2,
+        out_specs=(pl.BlockSpec(memory_space=pl.ANY),) * 2,
         scratch_shapes=list(scratch.values()),
         compiler_params=pltpu.CompilerParams(
             collective_id=0, has_side_effects=True, vmem_limit_bytes=56 * 1024 * 1024
@@ -667,7 +704,7 @@
             pltpu.VMEM((2 * CORES, depth // 2, s.width), F32),
             pltpu.SemaphoreType.DMA((2, 2 * CORES + 1)),
         ],
-    )(output, grads)
+    )(output, grads.reshape(CORES, depth, s.width))
 
 
 def solution(mesh):

time: 75.3 us -> 72.8 us (0.967)
  Pallas kernels: 74.4 us -> 71.9 us
    pallas_call x1, Pallas kernels: 72.4 us -> 69.9 us  [local(): pl.pallas_call(functools.partial(kernel, s, tuple(scratch)), out_shape=(j...]
where the time goes in v4:
time: 72.8 us; the launch traced here: 72.6 us
  Pallas kernels  71.9 us (99%)
    pallas_call x1, Pallas kernels, local(): pl.pallas_call(functools.partial(kernel, s, tuple(scratch)), out_shape=(j...  69.9 us
    pallas_call x1, Pallas kernels, local(): pl.pallas_call(finish, out_shape=(jax.ShapeDtypeStruct((nodes, s.width),...  2.06 us

profile of v4, /device:TPU:1, one launch (start us, length us, event | category | flops | bytes accessed | tf_op | source)
XLA Modules:
  0.0 72.6 jit_solution(10938507872725488197)
XLA Ops:
  0.6 69.9 %shard_map.94 = (bf16[1024,128]{1,0:T(8,128)(2,1)}, bf16[2,4,8,32,128]{4,3,2,1,0:T(8,128)(2,1)}) custom-call(bf16[1024,1024]{1,0:T(8,128)(2,1)} %feat_in.1, bf16[1024,128]{1,0:T(8,128)(2,1)} %w_self_in.1, bf16[1024,128]{1,0:T(8,128)(2,1)} %w_neigh_in.1, s32[8,1024]{1,0:T(8,128)} %bitcast.5, s32[4,1024]{1,0:T(4,128)} %bitcast.6, s32[4,1024]{1,0:T(4,128)} %bitcast.7, ...), custom_call_target="tpu_custom_call" | custom-call | tf_op jit(solution)/shard_map/pallas_call | solution.py:682
  70.5 2.1 %shard_map.95 = (bf16[1024,128]{1,0:T(8,128)(2,1)}, f32[1024,128]{1,0:T(8,128)}, f32[1024,128]{1,0:T(8,128)}) custom-call(bf16[1024,128]{1,0:T(8,128)(2,1)} %get-tuple-element.5.output_in, bf16[2,1024,128]{2,1,0:T(8,128)(2,1)} %bitcast.4), custom_call_target="tpu_custom_call" | custom-call | tf_op jit(solution)/shard_map/pallas_call | solution.py:696

commit v5 on v4

--- a/solution.py
+++ b/solution.py
@@ -272,9 +272,6 @@
     each(groups, lambda k: push_c(g_peer(k)[0], k).start())
     each(groups, lambda k: push_g(g_peer(k)[0], k).start())
 
-    inputs[5].wait()
-    loop(nodes // GROUP_ROWS, lambda i: build(r.locals_, i * GROUP_ROWS, GROUP_ROWS, r.nbr[...]))
-
     inputs[4].wait()
 
     def self_step(i):
@@ -317,6 +314,9 @@
 
     each(groups, lambda k: gather_g(k).start())
 
+    inputs[5].wait()
+    loop(nodes // GROUP_ROWS, lambda i: build(r.locals_, i * GROUP_ROWS, GROUP_ROWS, r.nbr[...]))
+
     def near_step(i):
         rows = pl.ds(pl.multiple_of(i * CHUNK, CHUNK), CHUNK)
         r.near[rows, :] = lax.dot_general(
@@ -351,7 +351,7 @@
 
     def activate(i):
         rows = slice(i * CHUNK, (i + 1) * CHUNK)
-        picks = lax.broadcasted_iota(jnp.int32, (2 * chunks, width), 0)
+        picks = lax.broadcasted_iota(jnp.int32, (CHUNK, width), 1)
         per_degree = 1.0 / r.degree[rows, :]
         pre = r.proj_self[rows, :] + r.near[rows, :] * per_degree
         sig = jax.nn.sigmoid(pre)
@@ -362,18 +362,12 @@
         r.act[rows, :] = act
         r.act_slope[rows, :] = act * slope
         r.cot_slope[rows, :] = cot * slope
-        sums = jnp.zeros((2 * chunks, CHUNK), F32)
+        sums = jnp.zeros((CHUNK, width), F32)
         for at, value in ((i, act * act), (chunks + i, act * cot)):
-            sums = sums + lax.dot_general(
-                jnp.where(picks == at, 1.0, 0.0),
-                value,
-                WIDE,
-                preferred_element_type=F32,
-                precision=lax.Precision.HIGHEST,
-            )
+            sums = jnp.where(picks == at, jnp.sum(value, axis=1, keepdims=True), sums)
         return sums
 
-    sums = jnp.zeros((2 * chunks, CHUNK), F32)
+    sums = jnp.zeros((CHUNK, width), F32)
     for i in range(1, chunks):
         pull(i)
         sums = sums + activate(i)
@@ -392,7 +386,7 @@
     count_in = jnp.sum(jnp.where(lane == sub + z * HUB_DEV, counts, 0.0), axis=1, keepdims=True)
     r.near[0:HUB_DEV, :] = r.near[0:HUB_DEV, :] + inflow
     r.degree[0:HUB_DEV, :] = r.degree[0:HUB_DEV, :] + count_in
-    r.sums[y] = sums + activate(0)
+    r.sums[y] = jnp.transpose(sums + activate(0))[0 : 2 * chunks]
 
     def col_sum(buf, row):
         return lambda k: copy(buf.at[y], buf.at[y], r.sems_y, row, k - 1, y_peer(k))
@@ -611,7 +605,7 @@
 
     def hand_over(k, px):
         piece = r.final.at[c, px]
-        return copy(piece, piece, r.sems_x, 1, k, partner)
+        return copy(piece, grads.at[c, px], r.sems_x, 1, k, partner)
 
     def keep(core, px):
         return pltpu.make_async_copy(r.final.at[core, px], grads.at[core, px], r.sems_o.at[core, px])
@@ -642,14 +636,8 @@
     loop(xs, lambda q: swap(q).wait_send())
     put_output.wait()
 
-    def take(k):
-        hand_over(k, 0).wait()
-        keep(1 - c, lax.rem(x + xs - k, xs)).start()
-
-    take(0)
-    each_near(xs, take)
-    for core in range(CORES):
-        loop(xs, lambda px: keep(core, px).wait())
+    loop(xs, lambda k: hand_over(k, 0).wait())
+    loop(xs, lambda px: keep(c, px).wait())
 
 
 def finish(output_in, grads_in, output_out, self_out, neigh_out, rows, low, high, sems):

time: 72.8 us -> 71.2 us (0.978)
  Pallas kernels: 71.9 us -> 70.3 us
    pallas_call x1, Pallas kernels: 69.9 us -> 68.3 us  [local(): pl.pallas_call(functools.partial(kernel, s, tuple(scratch)), out_shape=(j...]
where the time goes in v5:
time: 71.2 us; the launch traced here: 71 us
  Pallas kernels  70.3 us (99%)
    pallas_call x1, Pallas kernels, local(): pl.pallas_call(functools.partial(kernel, s, tuple(scratch)), out_shape=(j...  68.3 us
    pallas_call x1, Pallas kernels, local(): pl.pallas_call(finish, out_shape=(jax.ShapeDtypeStruct((nodes, s.width),...  2.06 us

profile of v5, /device:TPU:1, one launch (start us, length us, event | category | flops | bytes accessed | tf_op | source)
XLA Modules:
  0.0 71.0 jit_solution(15570958033329683359)
XLA Ops:
  0.6 68.3 %shard_map.94 = (bf16[1024,128]{1,0:T(8,128)(2,1)}, bf16[2,4,8,32,128]{4,3,2,1,0:T(8,128)(2,1)}) custom-call(bf16[1024,1024]{1,0:T(8,128)(2,1)} %feat_in.1, bf16[1024,128]{1,0:T(8,128)(2,1)} %w_self_in.1, bf16[1024,128]{1,0:T(8,128)(2,1)} %w_neigh_in.1, s32[8,1024]{1,0:T(8,128)} %bitcast.5, s32[4,1024]{1,0:T(4,128)} %bitcast.6, s32[4,1024]{1,0:T(4,128)} %bitcast.7, ...), custom_call_target="tpu_custom_call" | custom-call | tf_op jit(solution)/shard_map/pallas_call | solution.py:670
  68.9 2.1 %shard_map.95 = (bf16[1024,128]{1,0:T(8,128)(2,1)}, f32[1024,128]{1,0:T(8,128)}, f32[1024,128]{1,0:T(8,128)}) custom-call(bf16[1024,128]{1,0:T(8,128)(2,1)} %get-tuple-element.5.output_in, bf16[2,1024,128]{2,1,0:T(8,128)(2,1)} %bitcast.4), custom_call_target="tpu_custom_call" | custom-call | tf_op jit(solution)/shard_map/pallas_call | solution.py:684

commit v6 on v5

--- a/solution.py
+++ b/solution.py
@@ -257,8 +257,8 @@
 
     loop(groups, push_rows)
     pl.semaphore_wait(barrier, zs + groups + ys - 3)
+    each(groups, lambda k: push_p(g_peer(k)[0], k).start())
     each(zs, lambda k: gather_z(k).start())
-    each(groups, lambda k: push_p(g_peer(k)[0], k).start())
 
     def split_count(count):
         high = count.astype(BF16).astype(F32)

time: 71.2 us -> 71 us (level)
  no operation moved by 1% of the time
where the time goes in v6:
time: 71 us; the launch traced here: 70.8 us
  Pallas kernels  70.2 us (99%)
    pallas_call x1, Pallas kernels, local(): pl.pallas_call(functools.partial(kernel, s, tuple(scratch)), out_shape=(j...  68.1 us
    pallas_call x1, Pallas kernels, local(): pl.pallas_call(finish, out_shape=(jax.ShapeDtypeStruct((nodes, s.width),...  2.06 us

profile of v6, /device:TPU:1, one launch (start us, length us, event | category | flops | bytes accessed | tf_op | source)
XLA Modules:
  0.0 70.8 jit_solution(1779191668100031072)
XLA Ops:
  0.6 68.1 %shard_map.94 = (bf16[1024,128]{1,0:T(8,128)(2,1)}, bf16[2,4,8,32,128]{4,3,2,1,0:T(8,128)(2,1)}) custom-call(bf16[1024,1024]{1,0:T(8,128)(2,1)} %feat_in.1, bf16[1024,128]{1,0:T(8,128)(2,1)} %w_self_in.1, bf16[1024,128]{1,0:T(8,128)(2,1)} %w_neigh_in.1, s32[8,1024]{1,0:T(8,128)} %bitcast.5, s32[4,1024]{1,0:T(4,128)} %bitcast.6, s32[4,1024]{1,0:T(4,128)} %bitcast.7, ...), custom_call_target="tpu_custom_call" | custom-call | tf_op jit(solution)/shard_map/pallas_call | solution.py:670
  68.8 2.1 %shard_map.95 = (bf16[1024,128]{1,0:T(8,128)(2,1)}, f32[1024,128]{1,0:T(8,128)}, f32[1024,128]{1,0:T(8,128)}) custom-call(bf16[1024,128]{1,0:T(8,128)(2,1)} %get-tuple-element.5.output_in, bf16[2,1024,128]{2,1,0:T(8,128)(2,1)} %bitcast.4), custom_call_target="tpu_custom_call" | custom-call | tf_op jit(solution)/shard_map/pallas_call | solution.py:684
